TPU v7x, 32 devices: a whole 2x2x4 slice. The times are simulated.
32 devices in a mesh: tm: 4 (over y, core), lon: 4 (over z), head: 2 (over x).
Axes of the slice: x: 2, y: 2, z: 4, core: 2. Of those that a mesh axis runs over, the one named last changes fastest.
Arguments:
- query_field: bfloat16 [48, 8, 32, 1536], P('tm', None, 'lon', 'head'), may hold values from -8 to 8
- key_field: bfloat16 [48, 8, 32, 1536], P('tm', None, 'lon', 'head'), may hold values from -8 to 8
- value_field: bfloat16 [48, 8, 32, 1536], P('tm', None, 'lon', 'head'), may hold values from -6 to 6
- tile_offsets: int32 [8, 4], P('tm', 'lon'), may hold values from -1 to 1
- timesteps: int32 [8], P('tm'), may hold values from 0 to 999
- gate_weight: float32 [256, 1536], P(None, 'head'), may hold values from -0.375 to 0.375
Outputs:
- gated_field: bfloat16 [48, 8, 32, 1536], P('tm', None, 'lon', 'head')
Inputs may be any that keep to these rules, and one draw needn't show every extreme that they name: `tile_offsets`: the query tile (t, L) with shift s attends longitude tiles L + s - 1 to L + s + 1 around the loop.
All inputs are finite; a program needn't handle non-finite values.
Results may differ from a plain program's by a relative error of at most 0.0037.
Values may be sent and summed in bfloat16 or wider, within the bound.
A program may use at most 128 MiB of HBM per device.

v0:
```python
import math

import jax
import jax.numpy as jnp
from jax import lax
from jax.sharding import PartitionSpec as P

HD = 128
FREQ = 256
TILE_T = 6
TILE_H = 8
TILE_W = 8


def from_behind(block, axis, distance):
    devices = range(lax.axis_size(axis))
    route = [((i - distance) % len(devices), i) for i in devices]
    return lax.ppermute(block, axis, route)


def extended_2(x, sides, width):
    for axis, dim in sides:
        size, length = (lax.axis_size(axis), x.shape[dim])
        up = [(i, (i + 1) % size) for i in range(size - 1)]
        down = [(j, i) for i, j in up]
        last = lax.slice_in_dim(x, length - width, length, axis=dim)
        leading = lax.slice_in_dim(x, 0, width, axis=dim)
        before = lax.ppermute(last, axis, up)
        after = lax.ppermute(leading, axis, down)
        x = jnp.concatenate([before, x, after], axis=dim)
    return x


def start_at(*entries):
    return tuple((jnp.asarray(entry).astype(jnp.int32) for entry in entries))


def lon_extend(column_block):
    pieces = {}
    for shift_by in (2, 1, -1, -2):
        pieces[shift_by] = from_behind(column_block, "lon", shift_by)
    return jnp.concatenate([pieces[2], pieces[1], column_block, pieces[-1], pieces[-2]], axis=4)


def local(query_field, key_field, value_field, tile_offsets, timesteps, gate_weight):
    tiles_here = query_field.shape[0] // TILE_T
    features = query_field.shape[3]
    heads_here = features // HD
    tile_size = TILE_T * TILE_H * TILE_W
    tile_first = lax.axis_index("tm") * tiles_here
    time_count = tiles_here * lax.axis_size("tm")
    tiled_shape = (tiles_here, TILE_T, TILE_H, TILE_W, features)
    stacked = jnp.stack([key_field.reshape(tiled_shape), value_field.reshape(tiled_shape)], axis=1)
    rimmed = extended_2(stacked, (("tm", 0),), 1)
    extended = lon_extend(rimmed)
    half_freq = FREQ // 2
    frequencies = jnp.exp(-math.log(10000.0) * jnp.arange(half_freq, dtype=jnp.float32) / half_freq)
    angles = timesteps.astype(jnp.float32)[:, None] * frequencies[None, :]
    embedding = jnp.concatenate([jnp.cos(angles), jnp.sin(angles)], axis=1)
    gate_rows = jnp.dot(
        embedding, gate_weight, precision=lax.Precision.HIGHEST, preferred_element_type=jnp.float32
    )
    query_tiles = query_field.reshape(tiled_shape)
    inv_root = 1.0 / math.sqrt(HD)
    window_rows = 3 * TILE_T * TILE_H * 3 * TILE_W

    def one_pair(pair_index):
        tile_index = pair_index // heads_here
        head_index = pair_index % heads_here
        lon_shift = tile_offsets[tile_index, 0]
        window = lax.dynamic_slice(
            extended,
            start_at(tile_index, 0, 0, 0, (lon_shift + 1) * TILE_W, head_index * HD),
            (3, 2, TILE_T, TILE_H, 3 * TILE_W, HD),
        )
        key_rows = window[:, 0].reshape(window_rows, HD)
        value_rows = window[:, 1].reshape(window_rows, HD)
        query_rows = lax.dynamic_slice(
            query_tiles,
            start_at(tile_index, 0, 0, 0, head_index * HD),
            (1, TILE_T, TILE_H, TILE_W, HD),
        ).reshape(tile_size, HD)
        scores = (
            lax.dot_general(
                query_rows, key_rows, (((1,), (1,)), ((), ())), preferred_element_type=jnp.float32
            )
            * inv_root
        )
        window_times = tile_first + tile_index - 1 + jnp.arange(3, dtype=jnp.int32)
        usable = (window_times >= 0) & (window_times < time_count)
        scores = jnp.where(
            usable[None, :, None], scores.reshape(tile_size, 3, window_rows // 3), -1e30
        )
        scores = scores.reshape(tile_size, window_rows)
        row_max = jnp.max(scores, axis=1, keepdims=True)
        raised = jnp.exp(scores - row_max)
        totals = jnp.sum(raised, axis=1, keepdims=True)
        weights = raised.astype(jnp.bfloat16)
        weighted = jnp.dot(weights, value_rows, preferred_element_type=jnp.float32)
        gate_part = lax.dynamic_slice(gate_rows, start_at(tile_index, head_index * HD), (1, HD))
        return (weighted / totals * gate_part).astype(jnp.bfloat16)

    results = lax.map(one_pair, jnp.arange(tiles_here * heads_here, dtype=jnp.int32))
    results = results.reshape(tiles_here, heads_here, TILE_T, TILE_H, TILE_W, HD)
    results = jnp.transpose(results, (0, 2, 3, 4, 1, 5))
    return results.reshape(tiles_here * TILE_T, TILE_H, TILE_W, features)


def solution(mesh):
    return jax.shard_map(
        local,
        mesh=mesh,
        in_specs=(
            P("tm", None, "lon", "head"),
            P("tm", None, "lon", "head"),
            P("tm", None, "lon", "head"),
            P("tm", "lon"),
            P("tm"),
            P(None, "head"),
        ),
        out_specs=P("tm", None, "lon", "head"),
        check_vma=False,
    )
```

profile of v0, /device:TPU:9, one launch (start us, length us, event | category | flops | bytes accessed | tf_op | source)
XLA Modules:
  0.0 563.7 jit_solution(12347651341854909692)
XLA Ops:
  0.0 2.0 fusion.22
  2.0 3.7 collective-permute-start
  5.7 1.9 collective-permute-start.1
  7.6 11.2 %collective-permute-done = bf16[1,2,6,8,8,768]{5,4,3,2,1,0:T(8,128)(2,1)S(1)} collective-permute-done((bf16[1,2,6,8,8,768]{5,4,3,2,1,0:T(8,128)(2,1)S(1)}, bf16[1,2,6,8,8,768]{5,4,3,2,1,0:T(8,128)(2,1)S(1)}, u32[]{:S(2)}, u32[]{:S(2)}) %collective-permute-start) | collective-permute-done | bytes 1179680 | tf_op jit(solution)/shard_map/ppermute | solution.py:28
  18.8 4.8 collective-permute-done.1
  23.6 2.6 pad_maximum_fusion.1
  26.2 2.3 collective-permute-start.2
  28.6 1.5 collective-permute-start.4
  30.8 200.5 %collective-permute-done.2 = bf16[4,2,6,8,8,768]{5,4,3,2,1,0:T(8,128)(2,1)} collective-permute-done((bf16[4,2,6,8,8,768]{5,4,3,2,1,0:T(8,128)(2,1)}, bf16[4,2,6,8,8,768]{5,4,3,2,1,0:T(8,128)(2,1)}, u32[]{:S(2)}, u32[]{:S(2)}) %collective-permute-start.2) | collective-permute-done | bytes 4718624 | tf_op jit(solution)/shard_map/ppermute | solution.py:18
  231.3 2.6 constant_dynamic-update-slice_fusion.3
  234.0 187.1 %collective-permute-done.3 = bf16[4,2,6,8,8,768]{5,4,3,2,1,0:T(8,128)(2,1)} collective-permute-done((bf16[4,2,6,8,8,768]{5,4,3,2,1,0:T(8,128)(2,1)}, bf16[4,2,6,8,8,768]{5,4,3,2,1,0:T(8,128)(2,1)}, u32[]{:S(2)}, u32[]{:S(2)}) %collective-permute-start.3) | collective-permute-done | bytes 4718624 | tf_op jit(solution)/shard_map/ppermute | solution.py:18
  421.0 2.9 constant_dynamic-update-slice_fusion.2
  423.9 1.9 fusion.21
  425.9 2.7 constant_dynamic-update-slice_fusion.1
  428.6 2.9 constant_dynamic-update-slice_fusion
  431.4 7.8 %copy-done.3 = bf16[4,2,6,8,40,768]{5,4,3,2,1,0:T(8,128)(2,1)} copy-done((bf16[4,2,6,8,40,768]{5,4,3,2,1,0:T(8,128)(2,1)}, bf16[4,2,6,8,40,768]{5,4,3,2,1,0:T(8,128)(2,1)S(1)}, u32[]{:S(2)}) %copy-start.3) | copy-done | bytes 23592984
  439.3 122.0 %while.13 = (s32[]{:T(128)}, bf16[12,384,128]{2,1,0:T(8,128)(2,1)}, s32[12]{0:T(128)S(1)}, s32[]{:T(128)}, bf16[2,6,8,8,768]{4,3,2,1,0:T(8,128)(2,1)}, /*index=5...) while((s32[]{:T(128)}, bf16[12,384,128]{2,1,0:T(8,128)(2,1)}, ...), condition=%wide.region_3.4_spmd, body=%wide.region_0.3_spmd.sunk | while | flops 688913664 | bytes 21650988 | solution.py:103
  443.1 1.8 constant_dynamic-slice_fusion.6
  444.9 0.9 constant_dynamic-slice_fusion.7
  445.9 1.0 fusion.48
  447.9 1.5 fusion.50
  453.2 1.8 constant_dynamic-slice_fusion.6
  455.0 0.9 constant_dynamic-slice_fusion.7
  456.1 1.0 fusion.48
  458.0 1.5 fusion.50
  463.4 1.8 constant_dynamic-slice_fusion.6
  465.2 0.9 constant_dynamic-slice_fusion.7
  466.2 1.0 fusion.48
  468.2 1.5 fusion.50
  473.6 1.8 constant_dynamic-slice_fusion.6
  475.4 0.9 constant_dynamic-slice_fusion.7
  476.4 1.0 fusion.48
  478.4 1.5 fusion.50
  483.7 1.8 constant_dynamic-slice_fusion.6
  485.5 0.9 constant_dynamic-slice_fusion.7
  486.6 1.0 fusion.48
  488.5 1.6 fusion.50
  493.9 1.8 constant_dynamic-slice_fusion.6
  495.7 0.9 constant_dynamic-slice_fusion.7
  496.7 1.0 fusion.48
  498.7 1.5 fusion.50
  504.1 1.8 constant_dynamic-slice_fusion.6
  505.9 0.9 constant_dynamic-slice_fusion.7
  506.9 1.0 fusion.48
  508.9 1.5 fusion.50
  514.2 1.8 constant_dynamic-slice_fusion.6
  516.0 0.9 constant_dynamic-slice_fusion.7
  517.1 1.0 fusion.48
  519.0 1.5 fusion.50
  524.4 1.8 constant_dynamic-slice_fusion.6
  526.2 0.9 constant_dynamic-slice_fusion.7
  527.2 1.0 fusion.48
  529.2 1.5 fusion.50
  534.6 1.8 constant_dynamic-slice_fusion.6
  536.4 0.9 constant_dynamic-slice_fusion.7
  537.4 1.0 fusion.48
  539.4 1.5 fusion.50
  544.7 1.8 constant_dynamic-slice_fusion.6
  547.6 1.0 fusion.48
  549.5 1.5 fusion.50
  554.9 1.8 constant_dynamic-slice_fusion.6
  557.7 1.0 fusion.48
  559.7 1.6 fusion.50
  561.2 2.5 copy.7
  (112 shorter events, 29.2 us)
Async XLA Ops:
  0.0 30.4 %copy-start = (f32[256,768]{1,0:T(8,128)S(1)}, f32[256,768]{1,0:T(8,128)}, u32[]{:S(2)}) copy-start(f32[256,768]{1,0:T(8,128)} %param.13) | copy-start | bytes 2359300
  0.0 23.6 %copy-start.1 = (bf16[12,8,8,768]{3,2,1,0:T(8,128)(2,1)S(1)}, bf16[12,8,8,768]{3,2,1,0:T(8,128)(2,1)}, u32[]{:S(2)}) copy-start(bf16[12,8,8,768]{3,2,1,0:T(8,128)(2,1)} %param.9) | copy-start | bytes 3538948
  0.0 23.6 %copy-start.2 = (bf16[12,8,8,768]{3,2,1,0:T(8,128)(2,1)S(1)}, bf16[12,8,8,768]{3,2,1,0:T(8,128)(2,1)}, u32[]{:S(2)}) copy-start(bf16[12,8,8,768]{3,2,1,0:T(8,128)(2,1)} %param.10) | copy-start | bytes 3538948
  2.0 16.8 %collective-permute-start = (bf16[1,2,6,8,8,768]{5,4,3,2,1,0:T(8,128)(2,1)S(1)}, bf16[1,2,6,8,8,768]{5,4,3,2,1,0:T(8,128)(2,1)S(1)}, u32[]{:S(2)}, u32[]{:S(2)}) collective-permute-start(bf16[1,2,6,8,8,768]{5,4,3,2,1,0:T(8,128)(2,1)S(1)} %get-tuple-element.158), channel_id=1, source_target_pairs={{0,8},{8,16},{16,24},{1,9},{9,17},{17,25},{2,10},{10,18},{18,26},{... | collective-permute-start | bytes 3538952 | tf_op jit(solution)/shard_map/ppermute | solution.py:28
  5.7 24.3 %copy-start.7 = (s32[2]{0:T(128)S(1)}, s32[2]{0:T(128)}, u32[]{:S(2)}) copy-start(s32[2]{0:T(128)} %param.12) | copy-start | bytes 28
  5.7 17.9 %collective-permute-start.1 = (bf16[1,2,6,8,8,768]{5,4,3,2,1,0:T(8,128)(2,1)S(1)}, bf16[1,2,6,8,8,768]{5,4,3,2,1,0:T(8,128)(2,1)S(1)}, u32[]{:S(2)}, u32[]{:S(2)}) collective-permute-start(bf16[1,2,6,8,8,768]{5,4,3,2,1,0:T(8,128)(2,1)S(1)} %get-tuple-element.159), channel_id=1, source_target_pairs={{8,0},{16,8},{24,16},{9,1},{17,9},{25,17},{10,2},{18,10},{26,18},{... | collective-permute-start | bytes 3538952 | tf_op jit(solution)/shard_map/ppermute | solution.py:29
  18.8 7.4 %copy-start.4 = (bf16[1,2,6,8,8,768]{5,4,3,2,1,0:T(8,128)(2,1)}, bf16[1,2,6,8,8,768]{5,4,3,2,1,0:T(8,128)(2,1)S(1)}, u32[]{:S(2)}) copy-start(bf16[1,2,6,8,8,768]{5,4,3,2,1,0:T(8,128)(2,1)S(1)} %collective-permute-done) | copy-start | bytes 3538948
  23.6 4.9 copy-start.6
  26.2 205.1 %collective-permute-start.2 = (bf16[4,2,6,8,8,768]{5,4,3,2,1,0:T(8,128)(2,1)}, bf16[4,2,6,8,8,768]{5,4,3,2,1,0:T(8,128)(2,1)}, u32[]{:S(2)}, u32[]{:S(2)}) collective-permute-start(bf16[4,2,6,8,8,768]{5,4,3,2,1,0:T(8,128)(2,1)} %pad_maximum_fusion.1), channel_id=1, source_target_pairs={{4,0},{6,2},{0,4},{2,6},{5,1},{7,3},{1,5},{3,7},{12,8},{14,10},{8,... | collective-permute-start | bytes 14155784 | tf_op jit(solution)/shard_map/ppermute | solution.py:18
  28.5 392.5 %collective-permute-start.3 = (bf16[4,2,6,8,8,768]{5,4,3,2,1,0:T(8,128)(2,1)}, bf16[4,2,6,8,8,768]{5,4,3,2,1,0:T(8,128)(2,1)}, u32[]{:S(2)}, u32[]{:S(2)}) collective-permute-start(bf16[4,2,6,8,8,768]{5,4,3,2,1,0:T(8,128)(2,1)} %pad_maximum_fusion.1), channel_id=1, source_target_pairs={{6,0},{0,2},{2,4},{4,6},{7,1},{1,3},{3,5},{5,7},{14,8},{8,10},{10,... | collective-permute-start | bytes 14155784 | tf_op jit(solution)/shard_map/ppermute | solution.py:18
  28.6 397.3 %collective-permute-start.4 = (bf16[4,2,6,8,8,768]{5,4,3,2,1,0:T(8,128)(2,1)}, bf16[4,2,6,8,8,768]{5,4,3,2,1,0:T(8,128)(2,1)}, u32[]{:S(2)}, u32[]{:S(2)}) collective-permute-start(bf16[4,2,6,8,8,768]{5,4,3,2,1,0:T(8,128)(2,1)} %pad_maximum_fusion.1), channel_id=1, source_target_pairs={{2,0},{4,2},{6,4},{0,6},{3,1},{5,3},{7,5},{1,7},{10,8},{12,10},{14... | collective-permute-start | bytes 14155784 | tf_op jit(solution)/shard_map/ppermute | solution.py:18
  234.0 189.9 %copy-start.5 = (bf16[1,2,6,8,8,768]{5,4,3,2,1,0:T(8,128)(2,1)S(1)}, bf16[1,2,6,8,8,768]{5,4,3,2,1,0:T(8,128)(2,1)}, u32[]{:S(2)}) copy-start(bf16[1,2,6,8,8,768]{5,4,3,2,1,0:T(8,128)(2,1)} %copy-done.4) | copy-start | bytes 3538948
  428.5 10.7 %copy-start.8 = (s32[2,1]{0,1:T(1,128)S(1)}, s32[2,1]{0,1:T(1,128)}, u32[]{:S(2)}) copy-start(s32[2,1]{0,1:T(1,128)} %param.11) | copy-start | bytes 28
  431.4 7.8 %copy-start.3 = (bf16[4,2,6,8,40,768]{5,4,3,2,1,0:T(8,128)(2,1)}, bf16[4,2,6,8,40,768]{5,4,3,2,1,0:T(8,128)(2,1)S(1)}, u32[]{:S(2)}) copy-start(bf16[4,2,6,8,40,768]{5,4,3,2,1,0:T(8,128)(2,1)S(1)} %constant_dynamic-update-slice_fusion) | copy-start | bytes 70778880
where the time goes:
time: 566 us; the launch traced here: 564 us
  waiting for transfers between devices  404 us (71%)
  local copies, waits for them, and re-layouts  63.1 us (11%)
  loops' own time  31.9 us (6%)
  matrix products  31.4 us (6%)
  other arithmetic  24.2 us (4%)
  starting transfers between devices  9.4 us (2%)
    ppermute x3, waiting for transfers between devices, from_behind(): return lax.ppermute(block, axis, route)  388 us
    another operation x1, loops' own time, local(): lax.map(one_pair, jnp.arange(tiles_here * heads_here, dtype=jnp.int32))  31.9 us
    slice x12, local copies, waits for them, and re-layouts, one_pair(): key_rows = window[:, 0].reshape(window_rows, HD)  21.7 us
    dot_general x12, matrix products, one_pair(): weighted = jnp.dot(weights, value_rows, preferred_element_type=jnp.float32)  18.5 us
    unnamed x21, local copies, waits for them, and re-layouts  16 us
    dot_general x12, matrix products, one_pair(): lax.dot_general(query_rows, key_rows, (((1,), (1,)), ((), ())), preferred...  12.4 us
  transfers between devices with their start and end apart: 5, of which 4 were waited for; matrix products, arithmetic and copies ran while one was open for 1% of the time, Pallas kernels for 0%

commit v1 on v0

--- a/solution.py
+++ b/solution.py
@@ -1,8 +1,11 @@
+import functools
 import math
 
 import jax
 import jax.numpy as jnp
 from jax import lax
+from jax.experimental import pallas as pl
+from jax.experimental.pallas import tpu as pltpu
 from jax.sharding import PartitionSpec as P
 
 HD = 128
@@ -10,6 +13,206 @@
 TILE_T = 6
 TILE_H = 8
 TILE_W = 8
+TILE = TILE_T * TILE_H * TILE_W
+SCALE2 = math.log2(math.e) / math.sqrt(HD)
+NEG = -1e30
+CHUNK = 2
+STATS = 8
+
+
+def partial_kernel(times, columns, heads, flags_ref, q_ref, *refs):
+    kv_refs = refs[: 3 * columns]
+    o_ref, lse_ref, acc_ref, max_ref, stat_ref = refs[3 * columns :]
+    head = pl.program_id(0)
+    ones = jnp.ones((TILE, HD), jnp.bfloat16)
+    lanes = lax.broadcasted_iota(jnp.int32, (TILE, HD), 1)
+    prev_ok = flags_ref[columns * times] != 0
+    next_ok = flags_ref[columns * times + 1] != 0
+    for t in range(times):
+        acc_ref[...] = jnp.zeros_like(acc_ref)
+        max_ref[...] = jnp.full_like(max_ref, NEG)
+        for c in range(columns):
+            before, own, after = kv_refs[3 * c : 3 * c + 3]
+
+            @pl.when(flags_ref[c * times + t] != 0)
+            def _():
+                window = []
+                for w in range(t - 1, t + 2):
+                    if w < 0:
+                        window.append((before, 0, prev_ok))
+                    elif w >= times:
+                        window.append((after, 0, next_ok))
+                    else:
+                        window.append((own, w, None))
+                query = q_ref[t]
+                scores = []
+                for ref, w, ok in window:
+                    part = lax.dot_general(
+                        query, ref[0, w], (((1,), (1,)), ((), ())), preferred_element_type=jnp.float32
+                    )
+                    scores.append(part if ok is None else jnp.where(ok, part, NEG))
+                top = functools.reduce(jnp.maximum, scores)
+                top = jnp.max(top, axis=1, keepdims=True)
+                old = max_ref[...]
+                new = jnp.maximum(old, top)
+                max_ref[...] = new
+                fade = jnp.exp2((old - new) * SCALE2)
+                wide = jnp.concatenate([new] * (TILE // HD), axis=1)
+                total = jnp.concatenate([fade, fade], axis=1) * acc_ref[...]
+                for (ref, w, _), part in zip(window, scores):
+                    weights = jnp.exp2((part - wide) * SCALE2).astype(jnp.bfloat16)
+                    values = jnp.concatenate([ref[1, w], ones], axis=1)
+                    total += jnp.dot(weights, values, preferred_element_type=jnp.float32)
+                acc_ref[...] = total
+
+        sums = acc_ref[:, HD:]
+        some = sums > 0
+        safe = jnp.where(some, sums, 1.0)
+        o_ref[t] = (acc_ref[:, :HD] / safe).astype(o_ref.dtype)
+        lse = jnp.where(some, max_ref[...] * SCALE2 + jnp.log2(safe), NEG)
+        stat_ref[t] = jnp.where(lanes == head, lse, stat_ref[t])
+
+    @pl.when(head == heads - 1)
+    def _():
+        for t in range(times):
+            lse_ref[t] = jnp.transpose(stat_ref[t])[:STATS]
+
+
+def partial_attention(flags, query, columns, dtype):
+    times, _, features = query.shape
+    heads = features // HD
+    specs, operands = [], []
+    for column in columns:
+        for array in column:
+            shape = (2, array.shape[1], TILE, HD)
+            specs.append(pl.BlockSpec(shape, lambda h: (0, 0, 0, h)))
+            operands.append(array)
+    work = heads * times * len(columns) * 3 * TILE * TILE
+    return pl.pallas_call(
+        functools.partial(partial_kernel, times, len(columns), heads),
+        grid=(heads,),
+        out_shape=(
+            jax.ShapeDtypeStruct((times, TILE, features), dtype),
+            jax.ShapeDtypeStruct((times, STATS, TILE), jnp.float32),
+        ),
+        in_specs=[
+            pl.BlockSpec(memory_space=pltpu.SMEM),
+            pl.BlockSpec((times, TILE, HD), lambda h: (0, 0, h)),
+            *specs,
+        ],
+        out_specs=(
+            pl.BlockSpec((times, TILE, HD), lambda h: (0, 0, h)),
+            pl.BlockSpec((times, STATS, TILE), lambda h: (0, 0, 0)),
+        ),
+        scratch_shapes=[
+            pltpu.VMEM((TILE, 2 * HD), jnp.float32),
+            pltpu.VMEM((TILE, HD), jnp.float32),
+            pltpu.VMEM((times, TILE, HD), jnp.float32),
+        ],
+        compiler_params=pltpu.CompilerParams(vmem_limit_bytes=32 * 1024 * 1024),
+        cost_estimate=pl.CostEstimate(
+            flops=work * 8 * HD, bytes_accessed=2 * query.size * 8, transcendentals=work
+        ),
+    )(flags, query, *operands)
+
+
+def combine_kernel(times, heads, parts, gate_ref, *refs):
+    o_refs, lse_refs, out_ref = refs[:parts], refs[parts : 2 * parts], refs[2 * parts]
+    pad = jnp.zeros((HD - STATS, TILE), jnp.float32)
+    for t in range(times):
+        lses = [ref[t] for ref in lse_refs]
+        top = functools.reduce(jnp.maximum, lses)
+        raised = [jnp.exp2(lse - top) for lse in lses]
+        total = functools.reduce(jnp.add, raised)
+        shares = [jnp.transpose(jnp.concatenate([one / total, pad], axis=0)) for one in raised]
+        for h in range(heads):
+            columns = slice(h * HD, (h + 1) * HD)
+            result = functools.reduce(
+                jnp.add,
+                [
+                    share[:, h : h + 1] * ref[t, :, columns].astype(jnp.float32)
+                    for share, ref in zip(shares, o_refs)
+                ],
+            )
+            out_ref[t, :, columns] = (result * gate_ref[t : t + 1, columns]).astype(out_ref.dtype)
+
+
+def combine(gate, partials):
+    first = partials[0][0]
+    times, _, features = first.shape
+    return pl.pallas_call(
+        functools.partial(combine_kernel, times, features // HD, len(partials)),
+        out_shape=jax.ShapeDtypeStruct(first.shape, jnp.bfloat16),
+        compiler_params=pltpu.CompilerParams(vmem_limit_bytes=32 * 1024 * 1024),
+        cost_estimate=pl.CostEstimate(
+            flops=first.size * 8, bytes_accessed=first.size * 12, transcendentals=0
+        ),
+    )(gate, *[o for o, _ in partials], *[lse for _, lse in partials])
+
+
+def gate_of(timesteps, gate_weight):
+    half_freq = FREQ // 2
+    frequencies = jnp.exp(-math.log(10000.0) * jnp.arange(half_freq, dtype=jnp.float32) / half_freq)
+    angles = timesteps.astype(jnp.float32)[:, None] * frequencies[None, :]
+    embedding = jnp.concatenate([jnp.cos(angles), jnp.sin(angles)], axis=1)
+    return jnp.dot(
+        embedding, gate_weight, precision=lax.Precision.HIGHEST, preferred_element_type=jnp.float32
+    )
+
+
+def with_edges(kv):
+    size = lax.axis_size("tm")
+    up = [(i, i + 1) for i in range(size - 1)]
+    down = [(i + 1, i) for i in range(size - 1)]
+    before = lax.ppermute(kv[:, -1:], "tm", up)
+    after = lax.ppermute(kv[:, :1], "tm", down)
+    return before, kv, after
+
+
+def local_loop_of_four(query_field, key_field, value_field, tile_offsets, timesteps, gate_weight):
+    times = query_field.shape[0] // TILE_T
+    features = query_field.shape[3]
+    tiled = (times, TILE, features)
+    query, key, value = (x.reshape(tiled) for x in (query_field, key_field, value_field))
+    me = lax.axis_index("lon")
+    partner = me + 1 - 2 * (me % 2)
+    across = 3 - me
+    partners = [(0, 1), (1, 0), (2, 3), (3, 2)]
+    visits = [(0, 3), (3, 0), (1, 2), (2, 1)]
+    time_place = lax.axis_index("tm")
+    ends = jnp.stack([time_place > 0, time_place < lax.axis_size("tm") - 1])
+    offsets = tile_offsets[:, 0]
+    across_offsets = lax.ppermute(offsets, "lon", visits)
+
+    def used(column, home, shift):
+        return (column - home - shift + 8) % 4 != 2
+
+    def flags(*masks):
+        return jnp.concatenate([*masks, ends]).astype(jnp.int32)
+
+    always = jnp.ones((times,), jnp.bool_)
+    flags_own = flags(always)
+    flags_partner = flags(used(partner, me, offsets))
+    flags_visit = flags(used(me, across, across_offsets), used(partner, across, across_offsets))
+    gate_rows = gate_of(timesteps, gate_weight)
+    width = CHUNK * HD
+    pieces = []
+    for start in range(0, features, width):
+        part = slice(start, min(start + width, features))
+        own = jnp.stack([key[:, :, part], value[:, :, part]])
+        mine = query[:, :, part]
+        other = lax.ppermute(own, "lon", partners)
+        visitor = lax.ppermute(mine, "lon", visits)
+        pieces.append((part, mine, visitor, with_edges(own), other))
+    pieces = [(part, mine, visitor, own, with_edges(other)) for part, mine, visitor, own, other in pieces]
+    results = []
+    for part, mine, visitor, own, other in pieces:
+        sent = partial_attention(flags_visit, visitor, [own, other], jnp.bfloat16)
+        back = tuple(lax.ppermute(x, "lon", visits) for x in sent)
+        first = partial_attention(flags_own, mine, [own], jnp.float32)
+        second = partial_attention(flags_partner, mine, [other], jnp.float32)
+        results.append(combine(gate_rows[:, part], [first, second, back]))
+    return jnp.concatenate(results, axis=2).reshape(query_field.shape)
 
 
 def from_behind(block, axis, distance):
@@ -42,7 +245,7 @@
     return jnp.concatenate([pieces[2], pieces[1], column_block, pieces[-1], pieces[-2]], axis=4)
 
 
-def local(query_field, key_field, value_field, tile_offsets, timesteps, gate_weight):
+def local_any_loop(query_field, key_field, value_field, tile_offsets, timesteps, gate_weight):
     tiles_here = query_field.shape[0] // TILE_T
     features = query_field.shape[3]
     heads_here = features // HD
@@ -107,6 +310,7 @@
 
 
 def solution(mesh):
+    local = local_loop_of_four if mesh.shape["lon"] == 4 else local_any_loop
     return jax.shard_map(
         local,
         mesh=mesh,

time: 566 us -> 159 us (0.28)
  waiting for transfers between devices: 404 us -> 24.8 us
  local copies, waits for them, and re-layouts: 63.1 us -> 5.08 us
  starting transfers between devices: 9.4 us -> 65.7 us
  Pallas kernels: 0 us -> 51.6 us
  loops' own time: 31.9 us -> 0 us
  matrix products: 31.4 us -> 0.45 us
  other arithmetic: 24.2 us -> 9.24 us
    ppermute x5 -> x25, waiting for transfers between devices: 404 us -> 24.8 us  [the longest x3 15.7 us: local_loop_of_four(): visitor = lax.ppermute(mine, 'lon', visits)]
    ppermute x5 -> x25, starting transfers between devices: 9.4 us -> 65.7 us  [the longest x6 31.9 us: with_edges(): before = lax.ppermute(kv[:, -1:], 'tm', up)]
    pallas_call x0 -> x12, Pallas kernels: none -> 51.6 us  [the longest x9 48.3 us: partial_attention(): pl.pallas_call(functools.partial(partial_kernel, times, len(columns), hea...]
    another operation x1 -> x0, loops' own time: 31.9 us -> none  [local(): lax.map(one_pair, jnp.arange(tiles_here * heads_here, dtype=jnp.int32))]
    dot_general x25 -> x1, matrix products: 31.4 us -> 0.45 us  [gate_of(): jnp.dot(embedding, gate_weight, precision=lax.Precision.HIGHEST, preferre...]
    slice x12 -> x5, local copies, waits for them, and re-layouts: 21.7 us -> 2.39 us  [the longest x1 2.22 us: local_loop_of_four(): mine = query[:, :, part]]
    dynamic_slice x24 -> x0, local copies, waits for them, and re-layouts: 17.9 us -> none  [the longest x12 10.9 us: one_pair(): lax.dynamic_slice(query_tiles, start_at(tile_index, 0, 0, 0, head_index *...]
    unnamed x21 -> x18, local copies, waits for them, and re-layouts: 16 us -> 0.04 us
  transfers between devices with their start and end apart: 5 -> 25, of which waited for: 4 -> 4; matrix products, arithmetic and copies ran while one was open for 1% -> 9% of each run, Pallas kernels for 0% -> 32%
where the time goes in v1:
time: 159 us; the launch traced here: 157 us
  starting transfers between devices  65.7 us (41%)
  Pallas kernels  51.6 us (32%)
  waiting for transfers between devices  24.8 us (16%)
  other arithmetic  9.24 us (6%)
  local copies, waits for them, and re-layouts  5.08 us (3%)
    pallas_call x9, Pallas kernels, partial_attention(): pl.pallas_call(functools.partial(partial_kernel, times, len(columns), hea...  48.3 us
    ppermute x6, starting transfers between devices, with_edges(): before = lax.ppermute(kv[:, -1:], 'tm', up)  31.9 us
    ppermute x3, waiting for transfers between devices, local_loop_of_four(): visitor = lax.ppermute(mine, 'lon', visits)  15.7 us
    ppermute x6, starting transfers between devices, local_loop_of_four(): back = tuple((lax.ppermute(x, 'lon', visits) for x in sent))  15.1 us
    ppermute x6, starting transfers between devices, with_edges(): after = lax.ppermute(kv[:, :1], 'tm', down)  11.7 us
    ppermute x6, waiting for transfers between devices, local_loop_of_four(): back = tuple((lax.ppermute(x, 'lon', visits) for x in sent))  9.1 us
    another operation x6, other arithmetic, local_loop_of_four(): own = jnp.stack([key[:, :, part], value[:, :, part]])  6.53 us
    ppermute x3, starting transfers between devices, local_loop_of_four(): other = lax.ppermute(own, 'lon', partners)  4.1 us
  transfers between devices with their start and end apart: 25, of which 4 were waited for; matrix products, arithmetic and copies ran while one was open for 9% of the time, Pallas kernels for 32%

profile of v1, /device:TPU:9, one launch (start us, length us, event | category | flops | bytes accessed | tf_op | source)
XLA Modules:
  0.0 157.4 jit_solution(7600232394032672502)
XLA Ops:
  0.0 1.3 collective-permute-start.5
  1.3 2.6 %slice_bitcast_fusion.4 = (bf16[1,2,384,256]{3,2,1,0:T(8,128)(2,1)S(1)}, bf16[1,2,384,256]{3,2,1,0:T(8,128)(2,1)}, bf16[1,2,384,256]{3,2,1,0:T(8,128)(2,1)S(1)},...) fusion(bf16[2,384,768]{2,1,0:T(8,128)(2,1)} %bitcast.22, ...), kind=kLoop, calls=%fused_computation.26 | loop fusion | bytes 4718592 | tf_op jit(solution)/shard_map/stack | solution.py:202
  4.0 0.1 pad_maximum_fusion.1.refs_1_
  4.0 2.3 %collective-permute-start.2 = (bf16[2,2,384,256]{3,2,1,0:T(8,128)(2,1)S(1)}, bf16[2,2,384,256]{3,2,1,0:T(8,128)(2,1)S(1)}, u32[]{:S(2)}, u32[]{:S(2)}) collective-permute-start(bf16[2,2,384,256]{3,2,1,0:T(8,128)(2,1)S(1)} %pad_maximum_fusion.1.refs_1_), channel_id=1, source_target_pairs={{0,2},{2,0},{4,6},{6,4},{1,3},{3,1},{5,7},{7,5},{8,10},{10,8},{12,... | collective-permute-start | bytes 2359304 | tf_op jit(solution)/shard_map/ppermute | solution.py:204
  6.3 1.0 fusion.5
  7.3 4.3 %collective-permute-start = (bf16[2,1,384,256]{3,2,1,0:T(8,128)(2,1)}, bf16[2,1,384,256]{3,2,1,0:T(8,128)(2,1)}, u32[]{:S(2)}, u32[]{:S(2)}) collective-permute-start(bf16[2,1,384,256]{3,2,1,0:T(8,128)(2,1)} %get-tuple-element.53), channel_id=1, source_target_pairs={{0,8},{8,16},{16,24},{1,9},{9,17},{17,25},{2,10},{10,18},{18,26},{... | collective-permute-start | bytes 1179656 | tf_op jit(solution)/shard_map/ppermute | solution.py:167
  11.5 1.9 %collective-permute-start.1 = (bf16[2,1,384,256]{3,2,1,0:T(8,128)(2,1)}, bf16[2,1,384,256]{3,2,1,0:T(8,128)(2,1)}, u32[]{:S(2)}, u32[]{:S(2)}) collective-permute-start(bf16[2,1,384,256]{3,2,1,0:T(8,128)(2,1)} %get-tuple-element.52), channel_id=1, source_target_pairs={{8,0},{16,8},{24,16},{9,1},{17,9},{25,17},{10,2},{18,10},{26,18},{... | collective-permute-start | bytes 1179656 | tf_op jit(solution)/shard_map/ppermute | solution.py:168
  13.5 1.0 fusion.3
  14.4 1.9 %collective-permute-start.10 = (bf16[2,1,384,256]{3,2,1,0:T(8,128)(2,1)}, bf16[2,1,384,256]{3,2,1,0:T(8,128)(2,1)}, u32[]{:S(2)}, u32[]{:S(2)}) collective-permute-start(bf16[2,1,384,256]{3,2,1,0:T(8,128)(2,1)} %get-tuple-element.56), channel_id=1, source_target_pairs={{8,0},{16,8},{24,16},{9,1},{17,9},{25,17},{10,2},{18,10},{26,18},{... | collective-permute-start | bytes 1179656 | tf_op jit(solution)/shard_map/ppermute | solution.py:168
  16.4 1.1 pad_maximum_fusion.2.refs_1_
  17.5 0.0 copy-start.8
  17.5 0.0 copy-start.7
  17.5 2.2 %fusion.17 = (bf16[2,384,256]{2,1,0:T(8,128)(2,1)}, bf16[2,384,256]{2,1,0:T(8,128)(2,1)S(1)}, bf16[2,384,256]{2,1,0:T(8,128)(2,1)}) fusion(bf16[2,384,768]{2,1,0:T(8,128)(2,1)} %bitcast.21), kind=kLoop, calls=%fused_computation.54 | loop fusion | bytes 2359296 | tf_op jit(solution)/shard_map/slice | solution.py:203
  19.8 0.1 multiply_cosine_fusion
  19.9 0.5 fusion.6
  20.4 2.1 %pad_maximum_fusion.3.refs_1_ = bf16[2,2,384,256]{3,2,1,0:T(8,128)(2,1)} fusion(bf16[1,2,384,256]{3,2,1,0:T(8,128)(2,1)} %get-tuple-element.42, bf16[1,2,384,256]{3,2,1,0:T(8,128)(2,1)} %get-tuple-element.70), kind=kLoop, calls=%fused_computation.13 | loop fusion | flops 393216 | bytes 1572864 | tf_op jit(solution)/shard_map/stack | solution.py:202
  22.4 0.1 add_convert_fusion.1.flags_ref
  22.5 0.7 add_convert_fusion.flags_ref
  23.2 1.4 fusion.1
  24.6 3.6 %collective-permute-start.9 = (bf16[2,1,384,256]{3,2,1,0:T(8,128)(2,1)S(1)}, bf16[2,1,384,256]{3,2,1,0:T(8,128)(2,1)S(1)}, u32[]{:S(2)}, u32[]{:S(2)}) collective-permute-start(bf16[2,1,384,256]{3,2,1,0:T(8,128)(2,1)S(1)} %copy-done.6), channel_id=1, source_target_pairs={{0,8},{8,16},{16,24},{1,9},{9,17},{17,25},{2,10},{10,18},{18,26},{... | collective-permute-start | bytes 1179656 | tf_op jit(solution)/shard_map/ppermute | solution.py:167
  28.2 0.7 fusion.11
  28.9 0.1 collective-permute-start.11
  29.0 0.0 collective-permute-done.1.refs_2_
  29.0 3.1 %collective-permute-start.17 = (bf16[2,1,384,256]{3,2,1,0:T(8,128)(2,1)S(1)}, bf16[2,1,384,256]{3,2,1,0:T(8,128)(2,1)S(1)}, u32[]{:S(2)}, u32[]{:S(2)}) collective-permute-start(bf16[2,1,384,256]{3,2,1,0:T(8,128)(2,1)S(1)} %get-tuple-element.61), channel_id=1, source_target_pairs={{0,8},{8,16},{16,24},{1,9},{9,17},{17,25},{2,10},{10,18},{18,26},{... | collective-permute-start | bytes 1179656 | tf_op jit(solution)/shard_map/ppermute | solution.py:167
  32.1 1.9 %collective-permute-start.18 = (bf16[2,1,384,256]{3,2,1,0:T(8,128)(2,1)S(1)}, bf16[2,1,384,256]{3,2,1,0:T(8,128)(2,1)S(1)}, u32[]{:S(2)}, u32[]{:S(2)}) collective-permute-start(bf16[2,1,384,256]{3,2,1,0:T(8,128)(2,1)S(1)} %get-tuple-element.60), channel_id=1, source_target_pairs={{8,0},{16,8},{24,16},{9,1},{17,9},{25,17},{10,2},{18,10},{26,18},{... | collective-permute-start | bytes 1179656 | tf_op jit(solution)/shard_map/ppermute | solution.py:168
  34.1 0.1 add_convert_fusion.2.flags_ref
  34.2 6.3 %shard_map.64 = (f32[2,384,256]{2,1,0:T(8,128)S(1)}, f32[2,8,384]{2,1,0:T(8,128)S(1)}) custom-call(s32[4]{0:T(128)S(1)} %copy-done.4, bf16[2,384,256]{2,1,0:T(8,128)(2,1)S(1)} %copy-done.3, bf16[2,1,384,256]{3,2,1,0:T(8,128)(2,1)} %collective-permute-done.refs_0_, bf16[2,2,384,256]{3,2,1,0:T(8,128)(2,1)S(1)} %pad_maximum_fusion.1.refs_1_, ...), custom_call_target="tpu_custom_call" | custom-call | flops 1811939328 | bytes 3145728 | tf_op jit(solution)/shard_map/pallas_call | solution.py:91
  40.5 1.8 %collective-permute-start.19 = (bf16[2,2,384,256]{3,2,1,0:T(8,128)(2,1)S(1)}, bf16[2,2,384,256]{3,2,1,0:T(8,128)(2,1)S(1)}, u32[]{:S(2)}, u32[]{:S(2)}) collective-permute-start(bf16[2,2,384,256]{3,2,1,0:T(8,128)(2,1)S(1)} %copy-done.1), channel_id=1, source_target_pairs={{0,2},{2,0},{4,6},{6,4},{1,3},{3,1},{5,7},{7,5},{8,10},{10,8},{12,... | collective-permute-start | bytes 2359304 | tf_op jit(solution)/shard_map/ppermute | solution.py:204
  42.3 6.2 %shard_map.68 = (f32[2,384,256]{2,1,0:T(8,128)S(1)}, f32[2,8,384]{2,1,0:T(8,128)S(1)}) custom-call(s32[4]{0:T(128)S(1)} %copy-done.4, bf16[2,384,256]{2,1,0:T(8,128)(2,1)S(1)} %copy-done.2, bf16[2,1,384,256]{3,2,1,0:T(8,128)(2,1)S(1)} %collective-permute-done.9.refs_0_, bf16[2,2,384,256]{3,2,1,0:T(8,128)(2,1)S(1)} %pad_maximum_fusion.2.refs_1_, ...), custom_call_target="tpu_custom_call" | custom-call | flops 1811939328 | bytes 3145728 | tf_op jit(solution)/shard_map/pallas_call | solution.py:91
  48.5 0.0 collective-permute-done.17.refs_0_
  48.6 0.1 collective-permute-start.6
  48.6 1.4 collective-permute-start.14
  50.1 5.9 %shard_map.72 = (f32[2,384,256]{2,1,0:T(8,128)S(1)}, f32[2,8,384]{2,1,0:T(8,128)S(1)}) custom-call(s32[4]{0:T(128)S(1)} %copy-done.4, bf16[2,384,256]{2,1,0:T(8,128)(2,1)S(1)} %get-tuple-element.48.q_ref, bf16[2,1,384,256]{3,2,1,0:T(8,128)(2,1)S(1)} %collective-permute-done.17.refs_0_, bf16[2,2,384,256]{3,2,1,0:T(8,128)(2,1)S(1)} %copy-done.1, ...), custom_call_target="tpu_custom_call" | custom-call | flops 1811939328 | bytes 3145728 | tf_op jit(solution)/shard_map/pallas_call | solution.py:91
  56.0 0.0 collective-permute-done.2.refs_1_.refs_4_
  56.0 0.1 fusion.18
  56.0 4.5 %collective-permute-start.3 = (bf16[2,1,384,256]{3,2,1,0:T(8,128)(2,1)S(1)}, bf16[2,1,384,256]{3,2,1,0:T(8,128)(2,1)S(1)}, u32[]{:S(2)}, u32[]{:S(2)}) collective-permute-start(bf16[2,1,384,256]{3,2,1,0:T(8,128)(2,1)S(1)} %get-tuple-element.51), channel_id=1, source_target_pairs={{0,8},{8,16},{16,24},{1,9},{9,17},{17,25},{2,10},{10,18},{18,26},{... | collective-permute-start | bytes 1179656 | tf_op jit(solution)/shard_map/ppermute | solution.py:167
  60.5 0.0 collective-permute-done.11.refs_1_.refs_4_
  60.6 1.9 %collective-permute-start.4 = (bf16[2,1,384,256]{3,2,1,0:T(8,128)(2,1)S(1)}, bf16[2,1,384,256]{3,2,1,0:T(8,128)(2,1)S(1)}, u32[]{:S(2)}, u32[]{:S(2)}) collective-permute-start(bf16[2,1,384,256]{3,2,1,0:T(8,128)(2,1)S(1)} %get-tuple-element.50), channel_id=1, source_target_pairs={{8,0},{16,8},{24,16},{9,1},{17,9},{25,17},{10,2},{18,10},{26,18},{... | collective-permute-start | bytes 1179656 | tf_op jit(solution)/shard_map/ppermute | solution.py:168
  62.5 0.1 fusion.19
  62.6 3.6 %collective-permute-start.12 = (bf16[2,1,384,256]{3,2,1,0:T(8,128)(2,1)S(1)}, bf16[2,1,384,256]{3,2,1,0:T(8,128)(2,1)S(1)}, u32[]{:S(2)}, u32[]{:S(2)}) collective-permute-start(bf16[2,1,384,256]{3,2,1,0:T(8,128)(2,1)S(1)} %get-tuple-element.55), channel_id=1, source_target_pairs={{0,8},{8,16},{16,24},{1,9},{9,17},{17,25},{2,10},{10,18},{18,26},{... | collective-permute-start | bytes 1179656 | tf_op jit(solution)/shard_map/ppermute | solution.py:167
  66.2 1.9 %collective-permute-start.13 = (bf16[2,1,384,256]{3,2,1,0:T(8,128)(2,1)S(1)}, bf16[2,1,384,256]{3,2,1,0:T(8,128)(2,1)S(1)}, u32[]{:S(2)}, u32[]{:S(2)}) collective-permute-start(bf16[2,1,384,256]{3,2,1,0:T(8,128)(2,1)S(1)} %get-tuple-element.54), channel_id=1, source_target_pairs={{8,0},{16,8},{24,16},{9,1},{17,9},{25,17},{10,2},{18,10},{26,18},{... | collective-permute-start | bytes 1179656 | tf_op jit(solution)/shard_map/ppermute | solution.py:168
  68.1 0.1 fusion.20
  68.2 15.7 %collective-permute-done.14.q_ref = bf16[2,384,256]{2,1,0:T(8,128)(2,1)S(1)} collective-permute-done((bf16[2,384,256]{2,1,0:T(8,128)(2,1)S(1)}, bf16[2,384,256]{2,1,0:T(8,128)(2,1)S(1)}, u32[]{:S(2)}, u32[]{:S(2)}) %collective-permute-start.14) | collective-permute-done | bytes 393248 | tf_op jit(solution)/shard_map/ppermute | solution.py:205
  83.9 12.7 %collective-permute-start.20 = (bf16[2,1,384,256]{3,2,1,0:T(8,128)(2,1)S(1)}, bf16[2,1,384,256]{3,2,1,0:T(8,128)(2,1)S(1)}, u32[]{:S(2)}, u32[]{:S(2)}) collective-permute-start(bf16[2,1,384,256]{3,2,1,0:T(8,128)(2,1)S(1)} %get-tuple-element.59), channel_id=1, source_target_pairs={{0,8},{8,16},{16,24},{1,9},{9,17},{17,25},{2,10},{10,18},{18,26},{... | collective-permute-start | bytes 1179656 | tf_op jit(solution)/shard_map/ppermute | solution.py:167
  96.6 2.1 %collective-permute-start.21 = (bf16[2,1,384,256]{3,2,1,0:T(8,128)(2,1)S(1)}, bf16[2,1,384,256]{3,2,1,0:T(8,128)(2,1)S(1)}, u32[]{:S(2)}, u32[]{:S(2)}) collective-permute-start(bf16[2,1,384,256]{3,2,1,0:T(8,128)(2,1)S(1)} %get-tuple-element.58), channel_id=1, source_target_pairs={{8,0},{16,8},{24,16},{9,1},{17,9},{25,17},{10,2},{18,10},{26,18},{... | collective-permute-start | bytes 1179656 | tf_op jit(solution)/shard_map/ppermute | solution.py:168
  98.7 6.3 %shard_map.66 = (bf16[2,384,256]{2,1,0:T(8,128)(2,1)S(1)}, f32[2,8,384]{2,1,0:T(8,128)S(1)}) custom-call(s32[6]{0:T(128)S(1)} %add_convert_fusion.2.flags_ref, bf16[2,384,256]{2,1,0:T(8,128)(2,1)S(1)} %collective-permute-done.6.q_ref, bf16[2,1,384,256]{3,2,1,0:T(8,128)(2,1)} %collective-permute-done.refs_0_, ...), custom_call_target="tpu_custom_call" | custom-call | flops 3623878656 | bytes 3145728 | tf_op jit(solution)/shard_map/pallas_call | solution.py:91
  105.0 4.1 %collective-permute-start.7 = (bf16[2,384,256]{2,1,0:T(8,128)(2,1)S(1)}, bf16[2,384,256]{2,1,0:T(8,128)(2,1)S(1)}, u32[]{:S(2)}, u32[]{:S(2)}) collective-permute-start(bf16[2,384,256]{2,1,0:T(8,128)(2,1)S(1)} %get-tuple-element.25), channel_id=1, source_target_pairs={{0,6},{6,0},{2,4},{4,2},{1,7},{7,1},{3,5},{5,3},{8,14},{14,8},{10,... | collective-permute-start | bytes 1179656 | tf_op jit(solution)/shard_map/ppermute | solution.py:211
  109.1 0.1 collective-permute-start.8
  109.2 6.3 %shard_map.70 = (bf16[2,384,256]{2,1,0:T(8,128)(2,1)S(1)}, f32[2,8,384]{2,1,0:T(8,128)S(1)}) custom-call(s32[6]{0:T(128)S(1)} %add_convert_fusion.2.flags_ref, bf16[2,384,256]{2,1,0:T(8,128)(2,1)S(1)} %collective-permute-done.14.q_ref, bf16[2,1,384,256]{3,2,1,0:T(8,128)(2,1)S(1)} %collective-permute-done.9.refs_0_, ...), custom_call_target="tpu_custom_call" | custom-call | flops 3623878656 | bytes 3145728 | tf_op jit(solution)/shard_map/pallas_call | solution.py:91
  115.5 3.7 %collective-permute-start.15 = (bf16[2,384,256]{2,1,0:T(8,128)(2,1)S(1)}, bf16[2,384,256]{2,1,0:T(8,128)(2,1)S(1)}, u32[]{:S(2)}, u32[]{:S(2)}) collective-permute-start(bf16[2,384,256]{2,1,0:T(8,128)(2,1)S(1)} %get-tuple-element.31), channel_id=1, source_target_pairs={{0,6},{6,0},{2,4},{4,2},{1,7},{7,1},{3,5},{5,3},{8,14},{14,8},{10,... | collective-permute-start | bytes 1179656 | tf_op jit(solution)/shard_map/ppermute | solution.py:211
  119.2 0.1 collective-permute-start.16
  119.3 6.2 %shard_map.74 = (bf16[2,384,256]{2,1,0:T(8,128)(2,1)S(1)}, f32[2,8,384]{2,1,0:T(8,128)S(1)}) custom-call(s32[6]{0:T(128)S(1)} %add_convert_fusion.2.flags_ref, bf16[2,384,256]{2,1,0:T(8,128)(2,1)S(1)} %collective-permute-done.22.q_ref, bf16[2,1,384,256]{3,2,1,0:T(8,128)(2,1)S(1)} %collective-permute-done.17.refs_0_, bf16[2,2,384,256]{3,2,1,0:T(8,128)(2,1)S(1)} %copy-done.1, ...), custom_call_target="tpu_custom_call" | custom-call | flops 3623878656 | bytes 3145728 | tf_op jit(solution)/shard_map/pallas_call | solution.py:91
  125.5 3.5 %collective-permute-start.23 = (bf16[2,384,256]{2,1,0:T(8,128)(2,1)S(1)}, bf16[2,384,256]{2,1,0:T(8,128)(2,1)S(1)}, u32[]{:S(2)}, u32[]{:S(2)}) collective-permute-start(bf16[2,384,256]{2,1,0:T(8,128)(2,1)S(1)} %get-tuple-element.37), channel_id=1, source_target_pairs={{0,6},{6,0},{2,4},{4,2},{1,7},{7,1},{3,5},{5,3},{8,14},{14,8},{10,... | collective-permute-start | bytes 1179656 | tf_op jit(solution)/shard_map/ppermute | solution.py:211
  129.0 3.6 %shard_map.65 = (f32[2,384,256]{2,1,0:T(8,128)S(1)}, f32[2,8,384]{2,1,0:T(8,128)S(1)}) custom-call(s32[4]{0:T(128)S(1)} %add_convert_fusion.1.flags_ref, bf16[2,384,256]{2,1,0:T(8,128)(2,1)S(1)} %copy-done.3, bf16[2,1,384,256]{3,2,1,0:T(8,128)(2,1)S(1)} %collective-permute-done.3.refs_0_.refs_3_, ...), custom_call_target="tpu_custom_call" | custom-call | flops 1811939328 | bytes 3145728 | tf_op jit(solution)/shard_map/pallas_call | solution.py:91
  132.6 3.6 %shard_map.69 = (f32[2,384,256]{2,1,0:T(8,128)S(1)}, f32[2,8,384]{2,1,0:T(8,128)S(1)}) custom-call(s32[4]{0:T(128)S(1)} %add_convert_fusion.1.flags_ref, bf16[2,384,256]{2,1,0:T(8,128)(2,1)S(1)} %copy-done.2, bf16[2,1,384,256]{3,2,1,0:T(8,128)(2,1)S(1)} %collective-permute-done.12.refs_0_.refs_3_, ...), custom_call_target="tpu_custom_call" | custom-call | flops 1811939328 | bytes 3145728 | tf_op jit(solution)/shard_map/pallas_call | solution.py:91
  136.3 1.0 collective-permute-done.8.refs_5_
  137.3 3.7 %collective-permute-start.24 = (f32[2,8,384]{2,1,0:T(8,128)S(1)}, f32[2,8,384]{2,1,0:T(8,128)S(1)}, u32[]{:S(2)}, u32[]{:S(2)}) collective-permute-start(f32[2,8,384]{2,1,0:T(8,128)S(1)} %get-tuple-element.40), channel_id=1, source_target_pairs={{0,6},{6,0},{2,4},{4,2},{1,7},{7,1},{3,5},{5,3},{8,14},{14,8},{10,... | collective-permute-start | bytes 73736 | tf_op jit(solution)/shard_map/ppermute | solution.py:211
  140.9 3.9 %shard_map.73 = (f32[2,384,256]{2,1,0:T(8,128)S(1)}, f32[2,8,384]{2,1,0:T(8,128)S(1)}) custom-call(s32[4]{0:T(128)S(1)} %add_convert_fusion.1.flags_ref, bf16[2,384,256]{2,1,0:T(8,128)(2,1)S(1)} %get-tuple-element.48.q_ref, bf16[2,1,384,256]{3,2,1,0:T(8,128)(2,1)S(1)} %collective-permute-done.20.refs_0_.refs_3_, ...), custom_call_target="tpu_custom_call" | custom-call | flops 1811939328 | bytes 3145728 | tf_op jit(solution)/shard_map/pallas_call | solution.py:91
  144.8 1.1 shard_map.67
  145.9 0.3 collective-permute-done.16.refs_5_
  146.2 1.1 shard_map.71
  147.4 7.8 %collective-permute-done.24.refs_5_ = f32[2,8,384]{2,1,0:T(8,128)S(1)} collective-permute-done((f32[2,8,384]{2,1,0:T(8,128)S(1)}, f32[2,8,384]{2,1,0:T(8,128)S(1)}, u32[]{:S(2)}, u32[]{:S(2)}) %collective-permute-start.24) | collective-permute-done | bytes 24608 | tf_op jit(solution)/shard_map/ppermute | solution.py:211
  155.2 1.1 shard_map.75
  156.3 1.1 pad_maximum_fusion
  (39 shorter events, 0.1 us)
Async XLA Ops:
  0.0 19.9 %copy-start = (f32[256,768]{1,0:T(8,128)S(1)}, f32[256,768]{1,0:T(8,128)}, u32[]{:S(2)}) copy-start(f32[256,768]{1,0:T(8,128)} %param.11) | copy-start | bytes 2359300
  0.0 24.5 %collective-permute-start.5 = (s32[2]{0:T(128)}, s32[2]{0:T(128)}, u32[]{:S(2)}, u32[]{:S(2)}) collective-permute-start(s32[2]{0:T(128)} %bitcast.24), channel_id=1, source_target_pairs={{0,6},{6,0},{2,4},{4,2},{1,7},{7,1},{3,5},{5,3},{8,14},{14,8},{10,... | collective-permute-start | bytes 32 | tf_op jit(solution)/shard_map/ppermute | solution.py:185
  4.0 9.5 %copy-start.5 = (bf16[1,2,384,256]{3,2,1,0:T(8,128)(2,1)}, bf16[1,2,384,256]{3,2,1,0:T(8,128)(2,1)S(1)}, u32[]{:S(2)}) copy-start(bf16[1,2,384,256]{3,2,1,0:T(8,128)(2,1)S(1)} %get-tuple-element.69) | copy-start | bytes 1179652
  4.0 52.0 %collective-permute-start.2 = (bf16[2,2,384,256]{3,2,1,0:T(8,128)(2,1)S(1)}, bf16[2,2,384,256]{3,2,1,0:T(8,128)(2,1)S(1)}, u32[]{:S(2)}, u32[]{:S(2)}) collective-permute-start(bf16[2,2,384,256]{3,2,1,0:T(8,128)(2,1)S(1)} %pad_maximum_fusion.1.refs_1_), channel_id=1, source_target_pairs={{0,2},{2,0},{4,6},{6,4},{1,3},{3,1},{5,7},{7,5},{8,10},{10,8},{12,... | collective-permute-start | bytes 2359304 | tf_op jit(solution)/shard_map/ppermute | solution.py:204
  7.3 21.6 %collective-permute-start = (bf16[2,1,384,256]{3,2,1,0:T(8,128)(2,1)}, bf16[2,1,384,256]{3,2,1,0:T(8,128)(2,1)}, u32[]{:S(2)}, u32[]{:S(2)}) collective-permute-start(bf16[2,1,384,256]{3,2,1,0:T(8,128)(2,1)} %get-tuple-element.53), channel_id=1, source_target_pairs={{0,8},{8,16},{16,24},{1,9},{9,17},{17,25},{2,10},{10,18},{18,26},{... | collective-permute-start | bytes 1179656 | tf_op jit(solution)/shard_map/ppermute | solution.py:167
  11.5 17.5 %collective-permute-start.1 = (bf16[2,1,384,256]{3,2,1,0:T(8,128)(2,1)}, bf16[2,1,384,256]{3,2,1,0:T(8,128)(2,1)}, u32[]{:S(2)}, u32[]{:S(2)}) collective-permute-start(bf16[2,1,384,256]{3,2,1,0:T(8,128)(2,1)} %get-tuple-element.52), channel_id=1, source_target_pairs={{8,0},{16,8},{24,16},{9,1},{17,9},{25,17},{10,2},{18,10},{26,18},{... | collective-permute-start | bytes 1179656 | tf_op jit(solution)/shard_map/ppermute | solution.py:168
  14.4 17.7 %collective-permute-start.10 = (bf16[2,1,384,256]{3,2,1,0:T(8,128)(2,1)}, bf16[2,1,384,256]{3,2,1,0:T(8,128)(2,1)}, u32[]{:S(2)}, u32[]{:S(2)}) collective-permute-start(bf16[2,1,384,256]{3,2,1,0:T(8,128)(2,1)} %get-tuple-element.56), channel_id=1, source_target_pairs={{8,0},{16,8},{24,16},{9,1},{17,9},{25,17},{10,2},{18,10},{26,18},{... | collective-permute-start | bytes 1179656 | tf_op jit(solution)/shard_map/ppermute | solution.py:168
  17.5 2.3 %copy-start.8 = (s32[2,1]{0,1:T(1,128)S(1)}, s32[2,1]{0,1:T(1,128)}, u32[]{:S(2)}) copy-start(s32[2,1]{0,1:T(1,128)} %param.9) | copy-start | bytes 28
  17.5 2.3 %copy-start.7 = (s32[2]{0:T(128)S(1)}, s32[2]{0:T(128)}, u32[]{:S(2)}) copy-start(s32[2]{0:T(128)} %param.10) | copy-start | bytes 28
  23.2 1.4 copy-start.6
  23.2 11.0 %copy-start.3 = (bf16[2,384,256]{2,1,0:T(8,128)(2,1)S(1)}, bf16[2,384,256]{2,1,0:T(8,128)(2,1)}, u32[]{:S(2)}) copy-start(bf16[2,384,256]{2,1,0:T(8,128)(2,1)} %get-tuple-element.47.q_ref) | copy-start | bytes 1179652
  23.2 11.0 %copy-start.4 = (s32[4]{0:T(128)S(1)}, s32[4]{0:T(128)}, u32[]{:S(2)}) copy-start(s32[4]{0:T(128)} %add_convert_fusion.flags_ref) | copy-start | bytes 52
  24.6 15.9 %collective-permute-start.9 = (bf16[2,1,384,256]{3,2,1,0:T(8,128)(2,1)S(1)}, bf16[2,1,384,256]{3,2,1,0:T(8,128)(2,1)S(1)}, u32[]{:S(2)}, u32[]{:S(2)}) collective-permute-start(bf16[2,1,384,256]{3,2,1,0:T(8,128)(2,1)S(1)} %copy-done.6), channel_id=1, source_target_pairs={{0,8},{8,16},{16,24},{1,9},{9,17},{17,25},{2,10},{10,18},{18,26},{... | collective-permute-start | bytes 1179656 | tf_op jit(solution)/shard_map/ppermute | solution.py:167
  28.9 31.6 %collective-permute-start.11 = (bf16[2,2,384,256]{3,2,1,0:T(8,128)(2,1)S(1)}, bf16[2,2,384,256]{3,2,1,0:T(8,128)(2,1)S(1)}, u32[]{:S(2)}, u32[]{:S(2)}) collective-permute-start(bf16[2,2,384,256]{3,2,1,0:T(8,128)(2,1)S(1)} %pad_maximum_fusion.2.refs_1_), channel_id=1, source_target_pairs={{0,2},{2,0},{4,6},{6,4},{1,3},{3,1},{5,7},{7,5},{8,10},{10,8},{12,... | collective-permute-start | bytes 2359304 | tf_op jit(solution)/shard_map/ppermute | solution.py:204
  29.0 19.6 %collective-permute-start.17 = (bf16[2,1,384,256]{3,2,1,0:T(8,128)(2,1)S(1)}, bf16[2,1,384,256]{3,2,1,0:T(8,128)(2,1)S(1)}, u32[]{:S(2)}, u32[]{:S(2)}) collective-permute-start(bf16[2,1,384,256]{3,2,1,0:T(8,128)(2,1)S(1)} %get-tuple-element.61), channel_id=1, source_target_pairs={{0,8},{8,16},{16,24},{1,9},{9,17},{17,25},{2,10},{10,18},{18,26},{... | collective-permute-start | bytes 1179656 | tf_op jit(solution)/shard_map/ppermute | solution.py:167
  32.1 16.5 %collective-permute-start.18 = (bf16[2,1,384,256]{3,2,1,0:T(8,128)(2,1)S(1)}, bf16[2,1,384,256]{3,2,1,0:T(8,128)(2,1)S(1)}, u32[]{:S(2)}, u32[]{:S(2)}) collective-permute-start(bf16[2,1,384,256]{3,2,1,0:T(8,128)(2,1)S(1)} %get-tuple-element.60), channel_id=1, source_target_pairs={{8,0},{16,8},{24,16},{9,1},{17,9},{25,17},{10,2},{18,10},{26,18},{... | collective-permute-start | bytes 1179656 | tf_op jit(solution)/shard_map/ppermute | solution.py:168
  34.2 6.4 %copy-start.1 = (bf16[2,2,384,256]{3,2,1,0:T(8,128)(2,1)S(1)}, bf16[2,2,384,256]{3,2,1,0:T(8,128)(2,1)}, u32[]{:S(2)}) copy-start(bf16[2,2,384,256]{3,2,1,0:T(8,128)(2,1)} %pad_maximum_fusion.3.refs_1_) | copy-start | bytes 2359300
  34.2 8.1 %copy-start.2 = (bf16[2,384,256]{2,1,0:T(8,128)(2,1)S(1)}, bf16[2,384,256]{2,1,0:T(8,128)(2,1)}, u32[]{:S(2)}) copy-start(bf16[2,384,256]{2,1,0:T(8,128)(2,1)} %get-tuple-element.49.q_ref) | copy-start | bytes 1179652
  40.5 25.7 %collective-permute-start.19 = (bf16[2,2,384,256]{3,2,1,0:T(8,128)(2,1)S(1)}, bf16[2,2,384,256]{3,2,1,0:T(8,128)(2,1)S(1)}, u32[]{:S(2)}, u32[]{:S(2)}) collective-permute-start(bf16[2,2,384,256]{3,2,1,0:T(8,128)(2,1)S(1)} %copy-done.1), channel_id=1, source_target_pairs={{0,2},{2,0},{4,6},{6,4},{1,3},{3,1},{5,7},{7,5},{8,10},{10,8},{12,... | collective-permute-start | bytes 2359304 | tf_op jit(solution)/shard_map/ppermute | solution.py:204
  48.6 14.0 %collective-permute-start.6 = (bf16[2,384,256]{2,1,0:T(8,128)(2,1)S(1)}, bf16[2,384,256]{2,1,0:T(8,128)(2,1)S(1)}, u32[]{:S(2)}, u32[]{:S(2)}) collective-permute-start(bf16[2,384,256]{2,1,0:T(8,128)(2,1)S(1)} %copy-done.3), channel_id=1, source_target_pairs={{0,6},{6,0},{2,4},{4,2},{1,7},{7,1},{3,5},{5,3},{8,14},{14,8},{10,... | collective-permute-start | bytes 1179656 | tf_op jit(solution)/shard_map/ppermute | solution.py:205
  48.6 35.2 %collective-permute-start.14 = (bf16[2,384,256]{2,1,0:T(8,128)(2,1)S(1)}, bf16[2,384,256]{2,1,0:T(8,128)(2,1)S(1)}, u32[]{:S(2)}, u32[]{:S(2)}) collective-permute-start(bf16[2,384,256]{2,1,0:T(8,128)(2,1)S(1)} %copy-done.2), channel_id=1, source_target_pairs={{0,6},{6,0},{2,4},{4,2},{1,7},{7,1},{3,5},{5,3},{8,14},{14,8},{10,... | collective-permute-start | bytes 1179656 | tf_op jit(solution)/shard_map/ppermute | solution.py:205
  56.0 27.8 %collective-permute-start.3 = (bf16[2,1,384,256]{3,2,1,0:T(8,128)(2,1)S(1)}, bf16[2,1,384,256]{3,2,1,0:T(8,128)(2,1)S(1)}, u32[]{:S(2)}, u32[]{:S(2)}) collective-permute-start(bf16[2,1,384,256]{3,2,1,0:T(8,128)(2,1)S(1)} %get-tuple-element.51), channel_id=1, source_target_pairs={{0,8},{8,16},{16,24},{1,9},{9,17},{17,25},{2,10},{10,18},{18,26},{... | collective-permute-start | bytes 1179656 | tf_op jit(solution)/shard_map/ppermute | solution.py:167
  60.6 36.1 %collective-permute-start.4 = (bf16[2,1,384,256]{3,2,1,0:T(8,128)(2,1)S(1)}, bf16[2,1,384,256]{3,2,1,0:T(8,128)(2,1)S(1)}, u32[]{:S(2)}, u32[]{:S(2)}) collective-permute-start(bf16[2,1,384,256]{3,2,1,0:T(8,128)(2,1)S(1)} %get-tuple-element.50), channel_id=1, source_target_pairs={{8,0},{16,8},{24,16},{9,1},{17,9},{25,17},{10,2},{18,10},{26,18},{... | collective-permute-start | bytes 1179656 | tf_op jit(solution)/shard_map/ppermute | solution.py:168
  62.6 42.5 %collective-permute-start.12 = (bf16[2,1,384,256]{3,2,1,0:T(8,128)(2,1)S(1)}, bf16[2,1,384,256]{3,2,1,0:T(8,128)(2,1)S(1)}, u32[]{:S(2)}, u32[]{:S(2)}) collective-permute-start(bf16[2,1,384,256]{3,2,1,0:T(8,128)(2,1)S(1)} %get-tuple-element.55), channel_id=1, source_target_pairs={{0,8},{8,16},{16,24},{1,9},{9,17},{17,25},{2,10},{10,18},{18,26},{... | collective-permute-start | bytes 1179656 | tf_op jit(solution)/shard_map/ppermute | solution.py:167
  66.2 42.9 %collective-permute-start.13 = (bf16[2,1,384,256]{3,2,1,0:T(8,128)(2,1)S(1)}, bf16[2,1,384,256]{3,2,1,0:T(8,128)(2,1)S(1)}, u32[]{:S(2)}, u32[]{:S(2)}) collective-permute-start(bf16[2,1,384,256]{3,2,1,0:T(8,128)(2,1)S(1)} %get-tuple-element.54), channel_id=1, source_target_pairs={{8,0},{16,8},{24,16},{9,1},{17,9},{25,17},{10,2},{18,10},{26,18},{... | collective-permute-start | bytes 1179656 | tf_op jit(solution)/shard_map/ppermute | solution.py:168
  83.9 31.6 %collective-permute-start.22 = (bf16[2,384,256]{2,1,0:T(8,128)(2,1)S(1)}, bf16[2,384,256]{2,1,0:T(8,128)(2,1)S(1)}, u32[]{:S(2)}, u32[]{:S(2)}) collective-permute-start(bf16[2,384,256]{2,1,0:T(8,128)(2,1)S(1)} %get-tuple-element.48.q_ref), channel_id=1, source_target_pairs={{0,6},{6,0},{2,4},{4,2},{1,7},{7,1},{3,5},{5,3},{8,14},{14,8},{10,... | collective-permute-start | bytes 1179656 | tf_op jit(solution)/shard_map/ppermute | solution.py:205
  83.9 35.3 %collective-permute-start.20 = (bf16[2,1,384,256]{3,2,1,0:T(8,128)(2,1)S(1)}, bf16[2,1,384,256]{3,2,1,0:T(8,128)(2,1)S(1)}, u32[]{:S(2)}, u32[]{:S(2)}) collective-permute-start(bf16[2,1,384,256]{3,2,1,0:T(8,128)(2,1)S(1)} %get-tuple-element.59), channel_id=1, source_target_pairs={{0,8},{8,16},{16,24},{1,9},{9,17},{17,25},{2,10},{10,18},{18,26},{... | collective-permute-start | bytes 1179656 | tf_op jit(solution)/shard_map/ppermute | solution.py:167
  96.6 22.6 %collective-permute-start.21 = (bf16[2,1,384,256]{3,2,1,0:T(8,128)(2,1)S(1)}, bf16[2,1,384,256]{3,2,1,0:T(8,128)(2,1)S(1)}, u32[]{:S(2)}, u32[]{:S(2)}) collective-permute-start(bf16[2,1,384,256]{3,2,1,0:T(8,128)(2,1)S(1)} %get-tuple-element.58), channel_id=1, source_target_pairs={{8,0},{16,8},{24,16},{9,1},{17,9},{25,17},{10,2},{18,10},{26,18},{... | collective-permute-start | bytes 1179656 | tf_op jit(solution)/shard_map/ppermute | solution.py:168
  105.0 39.8 %collective-permute-start.7 = (bf16[2,384,256]{2,1,0:T(8,128)(2,1)S(1)}, bf16[2,384,256]{2,1,0:T(8,128)(2,1)S(1)}, u32[]{:S(2)}, u32[]{:S(2)}) collective-permute-start(bf16[2,384,256]{2,1,0:T(8,128)(2,1)S(1)} %get-tuple-element.25), channel_id=1, source_target_pairs={{0,6},{6,0},{2,4},{4,2},{1,7},{7,1},{3,5},{5,3},{8,14},{14,8},{10,... | collective-permute-start | bytes 1179656 | tf_op jit(solution)/shard_map/ppermute | solution.py:211
  109.1 28.2 %collective-permute-start.8 = (f32[2,8,384]{2,1,0:T(8,128)S(1)}, f32[2,8,384]{2,1,0:T(8,128)S(1)}, u32[]{:S(2)}, u32[]{:S(2)}) collective-permute-start(f32[2,8,384]{2,1,0:T(8,128)S(1)} %get-tuple-element.28), channel_id=1, source_target_pairs={{0,6},{6,0},{2,4},{4,2},{1,7},{7,1},{3,5},{5,3},{8,14},{14,8},{10,... | collective-permute-start | bytes 73736 | tf_op jit(solution)/shard_map/ppermute | solution.py:211
  115.5 30.8 %collective-permute-start.15 = (bf16[2,384,256]{2,1,0:T(8,128)(2,1)S(1)}, bf16[2,384,256]{2,1,0:T(8,128)(2,1)S(1)}, u32[]{:S(2)}, u32[]{:S(2)}) collective-permute-start(bf16[2,384,256]{2,1,0:T(8,128)(2,1)S(1)} %get-tuple-element.31), channel_id=1, source_target_pairs={{0,6},{6,0},{2,4},{4,2},{1,7},{7,1},{3,5},{5,3},{8,14},{14,8},{10,... | collective-permute-start | bytes 1179656 | tf_op jit(solution)/shard_map/ppermute | solution.py:211
  119.2 27.0 %collective-permute-start.16 = (f32[2,8,384]{2,1,0:T(8,128)S(1)}, f32[2,8,384]{2,1,0:T(8,128)S(1)}, u32[]{:S(2)}, u32[]{:S(2)}) collective-permute-start(f32[2,8,384]{2,1,0:T(8,128)S(1)} %get-tuple-element.34), channel_id=1, source_target_pairs={{0,6},{6,0},{2,4},{4,2},{1,7},{7,1},{3,5},{5,3},{8,14},{14,8},{10,... | collective-permute-start | bytes 73736 | tf_op jit(solution)/shard_map/ppermute | solution.py:211
  125.5 29.7 %collective-permute-start.23 = (bf16[2,384,256]{2,1,0:T(8,128)(2,1)S(1)}, bf16[2,384,256]{2,1,0:T(8,128)(2,1)S(1)}, u32[]{:S(2)}, u32[]{:S(2)}) collective-permute-start(bf16[2,384,256]{2,1,0:T(8,128)(2,1)S(1)} %get-tuple-element.37), channel_id=1, source_target_pairs={{0,6},{6,0},{2,4},{4,2},{1,7},{7,1},{3,5},{5,3},{8,14},{14,8},{10,... | collective-permute-start | bytes 1179656 | tf_op jit(solution)/shard_map/ppermute | solution.py:211
  137.3 17.9 %collective-permute-start.24 = (f32[2,8,384]{2,1,0:T(8,128)S(1)}, f32[2,8,384]{2,1,0:T(8,128)S(1)}, u32[]{:S(2)}, u32[]{:S(2)}) collective-permute-start(f32[2,8,384]{2,1,0:T(8,128)S(1)} %get-tuple-element.40), channel_id=1, source_target_pairs={{0,6},{6,0},{2,4},{4,2},{1,7},{7,1},{3,5},{5,3},{8,14},{14,8},{10,... | collective-permute-start | bytes 73736 | tf_op jit(solution)/shard_map/ppermute | solution.py:211

commit v2 on v0

--- a/solution.py
+++ b/solution.py
@@ -1,8 +1,11 @@
+import functools
 import math
 
 import jax
 import jax.numpy as jnp
 from jax import lax
+from jax.experimental import pallas as pl
+from jax.experimental.pallas import tpu as pltpu
 from jax.sharding import PartitionSpec as P
 
 HD = 128
@@ -10,6 +13,374 @@
 TILE_T = 6
 TILE_H = 8
 TILE_W = 8
+TILE = TILE_T * TILE_H * TILE_W
+SCALE2 = math.log2(math.e) / math.sqrt(HD)
+BIG = 1e30
+MESH = pl.DeviceIdType.MESH
+OWN, VISIT = 0, 1
+LON, QUERY, UP, DOWN, UP2, DOWN2, BACK, BACK_LSE = range(8)
+
+
+def attention_kernel(
+    times,
+    heads,
+    offset_ref,
+    key_ref,
+    value_ref,
+    query_ref,
+    gate_ref,
+    out_ref,
+    kv,
+    queries,
+    scores,
+    o_send,
+    o_back,
+    lse_send,
+    lse_back,
+    o_own,
+    lse_own,
+    staged,
+    cap_own,
+    cap_send,
+    cap_visit,
+    load_sem,
+    send_sem,
+    recv_sem,
+    cap_sem,
+    out_sem,
+):
+    me = lax.axis_index("lon")
+    partner = me + 1 - 2 * (me % 2)
+    across = 3 - me
+    place = lax.axis_index("tm")
+    last = lax.axis_size("tm") - 1
+    has_before, has_after = place > 0, place < last
+    end = times + 1
+
+    def lanes_of(h):
+        return pl.ds(pl.multiple_of(h * HD, HD), HD)
+
+    def loads(h):
+        inner = pl.ds(1, times)
+        return [
+            pltpu.make_async_copy(source.at[:, :, lanes_of(h)], target, load_sem.at[i, h])
+            for i, (source, target) in enumerate(
+                [
+                    (key_ref, kv.at[h, 0, 0, inner]),
+                    (value_ref, kv.at[h, 0, 1, inner]),
+                    (query_ref, queries.at[h, OWN]),
+                ]
+            )
+        ]
+
+    def remote(kind, h, source, target, device):
+        return pltpu.make_async_remote_copy(
+            src_ref=source,
+            dst_ref=target,
+            send_sem=send_sem.at[kind, h],
+            recv_sem=recv_sem.at[kind, h],
+            device_id=device,
+            device_id_type=MESH,
+        )
+
+    def lon_copy(h):
+        inner = pl.ds(1, times)
+        return remote(LON, h, kv.at[h, 0, :, inner], kv.at[h, 1, :, inner], {"lon": partner})
+
+    def query_copy(h):
+        return remote(QUERY, h, queries.at[h, OWN], queries.at[h, VISIT], {"lon": across})
+
+    def up_copy(h, c):
+        return remote((UP, UP2)[c], h, kv.at[h, c, :, times], kv.at[h, c, :, 0], {"tm": place + 1})
+
+    def down_copy(h, c):
+        return remote((DOWN, DOWN2)[c], h, kv.at[h, c, :, 1], kv.at[h, c, :, end], {"tm": place - 1})
+
+    def back_copy(h):
+        return remote(BACK, h, o_send.at[h], o_back.at[h], {"lon": across})
+
+    def back_lse_copy(h):
+        return remote(BACK_LSE, h, lse_send.at[h], lse_back.at[h], {"lon": across})
+
+    def out_copy(h):
+        return pltpu.make_async_copy(staged.at[h], out_ref.at[:, :, lanes_of(h)], out_sem.at[h])
+
+    cap_copy = pltpu.make_async_remote_copy(
+        src_ref=cap_send,
+        dst_ref=cap_visit,
+        send_sem=cap_sem.at[0],
+        recv_sem=cap_sem.at[1],
+        device_id={"lon": across},
+        device_id_type=MESH,
+    )
+
+    def load_all(h, carry):
+        for copy in loads(h):
+            copy.start()
+        return carry
+
+    lax.fori_loop(0, heads, load_all, 0)
+
+    barrier = pltpu.get_barrier_semaphore()
+    for neighbour in (partner, across):
+        pl.semaphore_signal(barrier, inc=1, device_id={"lon": neighbour}, device_id_type=MESH)
+
+    @pl.when(has_before)
+    def _():
+        pl.semaphore_signal(barrier, inc=1, device_id={"tm": place - 1}, device_id_type=MESH)
+
+    @pl.when(has_after)
+    def _():
+        pl.semaphore_signal(barrier, inc=1, device_id={"tm": place + 1}, device_id_type=MESH)
+
+    cap_own[...] = jnp.full_like(cap_own, BIG)
+    cap_send[...] = jnp.full_like(cap_send, BIG)
+    across_partner = across + 1 - 2 * (across % 2)
+    for t in range(times):
+        shift = offset_ref[t, 0]
+
+        def cap(column):
+            return jnp.where(lax.rem(column - me - shift + 8, 4) == 2, -BIG, BIG)
+
+        cap_own[2 * t + 1 : 2 * t + 2] = jnp.full((1, HD), cap(partner), jnp.float32)
+        cap_send[2 * t : 2 * t + 1] = jnp.full((1, HD), cap(across), jnp.float32)
+        cap_send[2 * t + 1 : 2 * t + 2] = jnp.full((1, HD), cap(across_partner), jnp.float32)
+
+    def blank(slot):
+        def step(h, carry):
+            for c in range(2):
+                for i in range(2):
+                    kv[h, c, i, slot] = jnp.zeros((TILE, HD), jnp.bfloat16)
+            return carry
+
+        lax.fori_loop(0, heads, step, 0)
+
+    @pl.when(jnp.logical_not(has_before))
+    def _():
+        blank(0)
+
+    @pl.when(jnp.logical_not(has_after))
+    def _():
+        blank(end)
+
+    pl.semaphore_wait(barrier, 2 + has_before.astype(jnp.int32) + has_after.astype(jnp.int32))
+    cap_copy.start()
+
+    def send_first(h):
+        for copy in loads(h):
+            copy.wait()
+        lon_copy(h).start()
+        query_copy(h).start()
+
+        @pl.when(has_after)
+        def _():
+            up_copy(h, 0).start()
+
+        @pl.when(has_before)
+        def _():
+            down_copy(h, 0).start()
+
+    def forward(h):
+        lon_copy(h).wait_recv()
+
+        @pl.when(has_after)
+        def _():
+            up_copy(h, 1).start()
+
+        @pl.when(has_before)
+        def _():
+            down_copy(h, 1).start()
+
+    send_first(0)
+    send_first(1)
+    cap_copy.wait()
+    forward(0)
+
+    before_cap = jnp.where(has_before, BIG, -BIG)
+    after_cap = jnp.where(has_after, BIG, -BIG)
+    ones = jnp.ones((TILE, HD), jnp.bfloat16)
+    wins = [(c, w) for c in range(2) for w in range(3)]
+
+    def score(h, whose, t, slot):
+        scaled = queries[h, whose, t].astype(jnp.float32) * SCALE2
+        high = scaled.astype(jnp.bfloat16)
+        low = (scaled - high.astype(jnp.float32)).astype(jnp.bfloat16)
+        query = jnp.concatenate([high, low], axis=1)
+        for i, (c, w) in enumerate(wins):
+            keys = kv[h, c, 0, t + w]
+            keys = jnp.concatenate([keys, keys], axis=1)
+            scores[slot, :, i * TILE : (i + 1) * TILE] = lax.dot_general(
+                query, keys, (((1,), (1,)), ((), ())), preferred_element_type=jnp.float32
+            )
+
+    def attend(h, whose, t, slot):
+        cap_ref = cap_visit if whose == VISIT else cap_own
+        caps, tops = [], []
+        for i, (c, w) in enumerate(wins):
+            limit = cap_ref[2 * t + c : 2 * t + c + 1]
+            if t + w == 0:
+                limit = jnp.minimum(limit, before_cap)
+            if t + w == end:
+                limit = jnp.minimum(limit, after_cap)
+            caps.append(limit)
+            part = [
+                scores[slot, :, i * TILE + j * HD : i * TILE + (j + 1) * HD] for j in range(TILE // HD)
+            ]
+            tops.append(jnp.minimum(functools.reduce(jnp.maximum, part), limit))
+        top = jnp.max(functools.reduce(jnp.maximum, tops), axis=1, keepdims=True)
+        total = None
+        for i, (c, w) in enumerate(wins):
+            base = jnp.maximum(top, -caps[i])
+            base = jnp.concatenate([base] * (TILE // HD), axis=1)
+            weights = jnp.exp2(scores[slot, :, i * TILE : (i + 1) * TILE] - base).astype(jnp.bfloat16)
+            values = jnp.concatenate([kv[h, c, 1, t + w], ones], axis=1)
+            part = jnp.dot(weights, values, preferred_element_type=jnp.float32)
+            total = part if total is None else total + part
+        sums = total[:, HD:]
+        return total[:, :HD] / sums, top + jnp.log2(sums)
+
+    def combine(h):
+        back_copy(h).wait_recv()
+        back_lse_copy(h).wait_recv()
+        pad = jnp.zeros((HD - 8, TILE), jnp.float32)
+        returned = jnp.transpose(jnp.concatenate([lse_back[h], pad], axis=0))
+        slot = h % 2
+        for t in range(times):
+            mine = lse_own[slot, t]
+            theirs = jnp.broadcast_to(returned[:, t : t + 1], mine.shape)
+            top = jnp.maximum(mine, theirs)
+            mine, theirs = jnp.exp2(mine - top), jnp.exp2(theirs - top)
+            gate = gate_ref[t : t + 1, lanes_of(h)]
+            mixed = o_own[slot, t] * mine + o_back[h, t].astype(jnp.float32) * theirs
+            staged[h, t] = (mixed / (mine + theirs) * gate).astype(jnp.bfloat16)
+        out_copy(h).start()
+
+    first_lane = lax.broadcasted_iota(jnp.int32, (TILE, HD), 1) == 0
+
+    def step(h, carry):
+        @pl.when(h + 2 < heads)
+        def _():
+            send_first(h + 2)
+
+        @pl.when(h + 1 < heads)
+        def _():
+            forward(h + 1)
+
+        query_copy(h).wait_recv()
+
+        @pl.when(has_before)
+        def _():
+            up_copy(h, 0).wait_recv()
+            up_copy(h, 1).wait_recv()
+
+        @pl.when(has_after)
+        def _():
+            down_copy(h, 0).wait_recv()
+            down_copy(h, 1).wait_recv()
+
+        slot = h % 2
+        score(h, VISIT, 0, 0)
+        score(h, VISIT, 1, 1)
+        o0, lse0 = attend(h, VISIT, 0, 0)
+        o_send[h, 0] = o0.astype(jnp.bfloat16)
+        score(h, OWN, 0, 0)
+        o1, lse1 = attend(h, VISIT, 1, 1)
+        o_send[h, 1] = o1.astype(jnp.bfloat16)
+        lse_send[h] = jnp.transpose(jnp.where(first_lane, lse0, lse1))[:8]
+        back_copy(h).start()
+        back_lse_copy(h).start()
+        score(h, OWN, 1, 1)
+        for t in range(times):
+            o, lse = attend(h, OWN, t, t)
+            o_own[slot, t] = o
+            lse_own[slot, t] = lse
+
+        @pl.when(h > 0)
+        def _():
+            combine(h - 1)
+
+        return carry
+
+    lax.fori_loop(0, heads, step, 0)
+    combine(heads - 1)
+
+    def finish(h, carry):
+        out_copy(h).wait()
+        for copy in (lon_copy(h), query_copy(h), back_copy(h), back_lse_copy(h)):
+            copy.wait_send()
+
+        @pl.when(has_after)
+        def _():
+            up_copy(h, 0).wait_send()
+            up_copy(h, 1).wait_send()
+
+        @pl.when(has_before)
+        def _():
+            down_copy(h, 0).wait_send()
+            down_copy(h, 1).wait_send()
+
+        return carry
+
+    lax.fori_loop(0, heads, finish, 0)
+
+
+def gate_of(timesteps, gate_weight):
+    half_freq = FREQ // 2
+    frequencies = jnp.exp(-math.log(10000.0) * jnp.arange(half_freq, dtype=jnp.float32) / half_freq)
+    angles = timesteps.astype(jnp.float32)[:, None] * frequencies[None, :]
+    embedding = jnp.concatenate([jnp.cos(angles), jnp.sin(angles)], axis=1)
+    return jnp.dot(
+        embedding, gate_weight, precision=lax.Precision.HIGHEST, preferred_element_type=jnp.float32
+    )
+
+
+def local_loop_of_four(query_field, key_field, value_field, tile_offsets, timesteps, gate_weight):
+    times = query_field.shape[0] // TILE_T
+    features = query_field.shape[3]
+    heads = features // HD
+    tiled = (times, TILE, features)
+    query, key, value = (x.reshape(tiled) for x in (query_field, key_field, value_field))
+    work = heads * times * 12 * TILE * TILE
+    per_head = (heads, times, TILE, HD)
+    result = pl.pallas_call(
+        functools.partial(attention_kernel, times, heads),
+        out_shape=jax.ShapeDtypeStruct(tiled, jnp.bfloat16),
+        in_specs=[
+            pl.BlockSpec(memory_space=pltpu.SMEM),
+            pl.BlockSpec(memory_space=pl.ANY),
+            pl.BlockSpec(memory_space=pl.ANY),
+            pl.BlockSpec(memory_space=pl.ANY),
+            pl.BlockSpec(memory_space=pltpu.VMEM),
+        ],
+        out_specs=pl.BlockSpec(memory_space=pl.ANY),
+        scratch_shapes=[
+            pltpu.VMEM((heads, 2, 2, times + 2, TILE, HD), jnp.bfloat16),
+            pltpu.VMEM((heads, 2, times, TILE, HD), jnp.bfloat16),
+            pltpu.VMEM((2, TILE, 6 * TILE), jnp.float32),
+            pltpu.VMEM(per_head, jnp.bfloat16),
+            pltpu.VMEM(per_head, jnp.bfloat16),
+            pltpu.VMEM((heads, 8, TILE), jnp.float32),
+            pltpu.VMEM((heads, 8, TILE), jnp.float32),
+            pltpu.VMEM((2, times, TILE, HD), jnp.float32),
+            pltpu.VMEM((2, times, TILE, HD), jnp.float32),
+            pltpu.VMEM(per_head, jnp.bfloat16),
+            pltpu.VMEM((8, HD), jnp.float32),
+            pltpu.VMEM((8, HD), jnp.float32),
+            pltpu.VMEM((8, HD), jnp.float32),
+            pltpu.SemaphoreType.DMA((3, heads)),
+            pltpu.SemaphoreType.DMA((8, heads)),
+            pltpu.SemaphoreType.DMA((8, heads)),
+            pltpu.SemaphoreType.DMA((2,)),
+            pltpu.SemaphoreType.DMA((heads,)),
+        ],
+        compiler_params=pltpu.CompilerParams(
+            collective_id=0, has_side_effects=True, vmem_limit_bytes=52 * 1024 * 1024
+        ),
+        cost_estimate=pl.CostEstimate(
+            flops=work * 4 * HD, bytes_accessed=8 * query.size, transcendentals=work
+        ),
+    )(tile_offsets, key, value, query, gate_of(timesteps, gate_weight))
+    return result.reshape(query_field.shape)
 
 
 def from_behind(block, axis, distance):
@@ -42,7 +413,7 @@
     return jnp.concatenate([pieces[2], pieces[1], column_block, pieces[-1], pieces[-2]], axis=4)
 
 
-def local(query_field, key_field, value_field, tile_offsets, timesteps, gate_weight):
+def local_any_loop(query_field, key_field, value_field, tile_offsets, timesteps, gate_weight):
     tiles_here = query_field.shape[0] // TILE_T
     features = query_field.shape[3]
     heads_here = features // HD
@@ -107,6 +478,7 @@
 
 
 def solution(mesh):
+    local = local_loop_of_four if mesh.shape["lon"] == 4 else local_any_loop
     return jax.shard_map(
         local,
         mesh=mesh,

time: 566 us -> 123 us (0.22)
  waiting for transfers between devices: 404 us -> 0 us
  Pallas kernels: 0 us -> 119 us
  local copies, waits for them, and re-layouts: 63.1 us -> 1.77 us
  loops' own time: 31.9 us -> 0 us
  matrix products: 31.4 us -> 0.45 us
  other arithmetic: 24.2 us -> 0.85 us
  starting transfers between devices: 9.4 us -> 0 us
    ppermute x5 -> x0, waiting for transfers between devices: 404 us -> none  [the longest x3 388 us: from_behind(): return lax.ppermute(block, axis, route)]
    pallas_call x0 -> x1, Pallas kernels: none -> 119 us  [local_loop_of_four(): pl.pallas_call(functools.partial(attention_kernel, times, heads), out_sha...]
    another operation x1 -> x0, loops' own time: 31.9 us -> none  [local(): lax.map(one_pair, jnp.arange(tiles_here * heads_here, dtype=jnp.int32))]
    dot_general x25 -> x1, matrix products: 31.4 us -> 0.45 us  [gate_of(): jnp.dot(embedding, gate_weight, precision=lax.Precision.HIGHEST, preferre...]
    slice x12 -> x0, local copies, waits for them, and re-layouts: 21.7 us -> none  [one_pair(): key_rows = window[:, 0].reshape(window_rows, HD)]
    dynamic_slice x24 -> x0, local copies, waits for them, and re-layouts: 17.9 us -> none  [the longest x12 10.9 us: one_pair(): lax.dynamic_slice(query_tiles, start_at(tile_index, 0, 0, 0, head_index *...]
    unnamed x21 -> x4, local copies, waits for them, and re-layouts: 16 us -> 1.77 us
    reduce_sum x12 -> x0, other arithmetic: 10.3 us -> none  [one_pair(): totals = jnp.sum(raised, axis=1, keepdims=True)]
  transfers between devices with their start and end apart: 5 -> 0, of which waited for: 4 -> 0; matrix products, arithmetic and copies ran while one was open for 1% -> 0% of each run, Pallas kernels for 0% -> 0%
where the time goes in v2:
time: 123 us
  Pallas kernels  119 us (97%)
  local copies, waits for them, and re-layouts  1.77 us (1%)
    pallas_call x1, Pallas kernels, local_loop_of_four(): pl.pallas_call(functools.partial(attention_kernel, times, heads), out_sha...  119 us

profile of v2, /device:TPU:9, one launch (start us, length us, event | category | flops | bytes accessed | tf_op | source)
XLA Modules:
  0.0 122.6 jit_solution(13098103175893261320)
XLA Ops:
  0.0 0.0 copy-start
  0.0 0.7 convert_element_type.3
  0.7 0.7 copy.7.offset_ref
  1.5 0.1 multiply_cosine_fusion
  1.6 0.0 copy-done
  1.6 0.5 fusion.gate_ref
  2.1 119.5 %shard_map.64 = bf16[2,384,768]{2,1,0:T(8,128)(2,1)S(1)} custom-call(s32[2,1]{1,0:T(2,128)S(1)} %copy.7.offset_ref, bf16[2,384,768]{2,1,0:T(8,128)(2,1)} %bitcast.6, bf16[2,384,768]{2,1,0:T(8,128)(2,1)} %bitcast.7, bf16[2,384,768]{2,1,0:T(8,128)(2,1)} %bitcast.8, f32[2,768]{1,0:T(2,128)S(1)} %fusion.gate_ref), custom_call_target="tpu_custom_call" | custom-call | flops 10871635968 | bytes 4718592 | tf_op jit(solution)/shard_map/pallas_call | solution.py:345
  121.6 1.0 copy.9
  (1 shorter events, 0.0 us)
Async XLA Ops:
  0.0 1.6 %copy-start = (f32[256,768]{1,0:T(8,128)S(1)}, f32[256,768]{1,0:T(8,128)}, u32[]{:S(2)}) copy-start(f32[256,768]{1,0:T(8,128)} %param.11) | copy-start | bytes 2359300

commit v3 on v2

--- a/solution.py
+++ b/solution.py
@@ -18,7 +18,7 @@
 BIG = 1e30
 MESH = pl.DeviceIdType.MESH
 OWN, VISIT = 0, 1
-LON, QUERY, UP, DOWN, UP2, DOWN2, BACK, BACK_LSE = range(8)
+LON, QUERY, UP, DOWN, UP2, DOWN2, BACK_LSE, BACK = range(8)
 
 
 def attention_kernel(
@@ -60,17 +60,16 @@
     def lanes_of(h):
         return pl.ds(pl.multiple_of(h * HD, HD), HD)
 
-    def loads(h):
+    def loads(h, picked=(0, 1, 2)):
         inner = pl.ds(1, times)
+        pairs = [
+            (key_ref, kv.at[h, 0, 0, inner]),
+            (value_ref, kv.at[h, 0, 1, inner]),
+            (query_ref, queries.at[h, OWN]),
+        ]
         return [
-            pltpu.make_async_copy(source.at[:, :, lanes_of(h)], target, load_sem.at[i, h])
-            for i, (source, target) in enumerate(
-                [
-                    (key_ref, kv.at[h, 0, 0, inner]),
-                    (value_ref, kv.at[h, 0, 1, inner]),
-                    (query_ref, queries.at[h, OWN]),
-                ]
-            )
+            pltpu.make_async_copy(pairs[i][0].at[:, :, lanes_of(h)], pairs[i][1], load_sem.at[i, h])
+            for i in picked
         ]
 
     def remote(kind, h, source, target, device):
@@ -96,8 +95,8 @@
     def down_copy(h, c):
         return remote((DOWN, DOWN2)[c], h, kv.at[h, c, :, 1], kv.at[h, c, :, end], {"tm": place - 1})
 
-    def back_copy(h):
-        return remote(BACK, h, o_send.at[h], o_back.at[h], {"lon": across})
+    def back_copy(h, t):
+        return remote(BACK + t, h, o_send.at[h, t], o_back.at[h, t], {"lon": across})
 
     def back_lse_copy(h):
         return remote(BACK_LSE, h, lse_send.at[h], lse_back.at[h], {"lon": across})
@@ -166,11 +165,24 @@
     pl.semaphore_wait(barrier, 2 + has_before.astype(jnp.int32) + has_after.astype(jnp.int32))
     cap_copy.start()
 
+    inner = (me == 1) | (me == 2)
+
+    def send_queries(h, carry):
+        query_copy(h).start()
+        return carry
+
+    def wait_queries(h, carry):
+        loads(h, (2,))[0].wait()
+        return carry
+
     def send_first(h):
-        for copy in loads(h):
+        for copy in loads(h, (0, 1)):
             copy.wait()
         lon_copy(h).start()
-        query_copy(h).start()
+
+        @pl.when(jnp.logical_not(inner))
+        def _():
+            query_copy(h).start()
 
         @pl.when(has_after)
         def _():
@@ -191,7 +203,13 @@
         def _():
             down_copy(h, 1).start()
 
+    lax.fori_loop(0, heads, wait_queries, 0)
     send_first(0)
+
+    @pl.when(inner)
+    def _():
+        lax.fori_loop(0, heads, send_queries, 0)
+
     send_first(1)
     cap_copy.wait()
     forward(0)
@@ -240,9 +258,10 @@
         return total[:, :HD] / sums, top + jnp.log2(sums)
 
     def combine(h):
-        back_copy(h).wait_recv()
+        for t in range(times):
+            back_copy(h, t).wait_recv()
         back_lse_copy(h).wait_recv()
-        pad = jnp.zeros((HD - 8, TILE), jnp.float32)
+        pad = jnp.zeros((HD - times, TILE), jnp.float32)
         returned = jnp.transpose(jnp.concatenate([lse_back[h], pad], axis=0))
         slot = h % 2
         for t in range(times):
@@ -262,10 +281,6 @@
         def _():
             send_first(h + 2)
 
-        @pl.when(h + 1 < heads)
-        def _():
-            forward(h + 1)
-
         query_copy(h).wait_recv()
 
         @pl.when(has_before)
@@ -283,12 +298,18 @@
         score(h, VISIT, 1, 1)
         o0, lse0 = attend(h, VISIT, 0, 0)
         o_send[h, 0] = o0.astype(jnp.bfloat16)
+        back_copy(h, 0).start()
         score(h, OWN, 0, 0)
         o1, lse1 = attend(h, VISIT, 1, 1)
         o_send[h, 1] = o1.astype(jnp.bfloat16)
-        lse_send[h] = jnp.transpose(jnp.where(first_lane, lse0, lse1))[:8]
-        back_copy(h).start()
+        lse_send[h] = jnp.transpose(jnp.where(first_lane, lse0, lse1))[:times]
+        back_copy(h, 1).start()
         back_lse_copy(h).start()
+
+        @pl.when(h + 1 < heads)
+        def _():
+            forward(h + 1)
+
         score(h, OWN, 1, 1)
         for t in range(times):
             o, lse = attend(h, OWN, t, t)
@@ -306,7 +327,8 @@
 
     def finish(h, carry):
         out_copy(h).wait()
-        for copy in (lon_copy(h), query_copy(h), back_copy(h), back_lse_copy(h)):
+        backs = [back_copy(h, t) for t in range(times)]
+        for copy in (lon_copy(h), query_copy(h), back_lse_copy(h), *backs):
             copy.wait_send()
 
         @pl.when(has_after)
@@ -359,8 +381,8 @@
             pltpu.VMEM((2, TILE, 6 * TILE), jnp.float32),
             pltpu.VMEM(per_head, jnp.bfloat16),
             pltpu.VMEM(per_head, jnp.bfloat16),
-            pltpu.VMEM((heads, 8, TILE), jnp.float32),
-            pltpu.VMEM((heads, 8, TILE), jnp.float32),
+            pltpu.VMEM((heads, times, TILE), jnp.float32),
+            pltpu.VMEM((heads, times, TILE), jnp.float32),
             pltpu.VMEM((2, times, TILE, HD), jnp.float32),
             pltpu.VMEM((2, times, TILE, HD), jnp.float32),
             pltpu.VMEM(per_head, jnp.bfloat16),
@@ -368,8 +390,8 @@
             pltpu.VMEM((8, HD), jnp.float32),
             pltpu.VMEM((8, HD), jnp.float32),
             pltpu.SemaphoreType.DMA((3, heads)),
-            pltpu.SemaphoreType.DMA((8, heads)),
-            pltpu.SemaphoreType.DMA((8, heads)),
+            pltpu.SemaphoreType.DMA((7 + times, heads)),
+            pltpu.SemaphoreType.DMA((7 + times, heads)),
             pltpu.SemaphoreType.DMA((2,)),
             pltpu.SemaphoreType.DMA((heads,)),
         ],

time: 123 us -> 117 us (0.951)
  Pallas kernels: 119 us -> 114 us
    pallas_call x1, Pallas kernels: 119 us -> 114 us  [local_loop_of_four(): pl.pallas_call(functools.partial(attention_kernel, times, heads), out_sha...]
where the time goes in v3:
time: 117 us
  Pallas kernels  114 us (97%)
  local copies, waits for them, and re-layouts  1.77 us (2%)
    pallas_call x1, Pallas kernels, local_loop_of_four(): pl.pallas_call(functools.partial(attention_kernel, times, heads), out_sha...  114 us

profile of v3, /device:TPU:9, one launch (start us, length us, event | category | flops | bytes accessed | tf_op | source)
XLA Modules:
  0.0 117.0 jit_solution(11062177354952163899)
XLA Ops:
  0.0 0.0 copy-start
  0.0 0.7 convert_element_type.3
  0.7 0.7 copy.7.offset_ref
  1.5 0.1 multiply_cosine_fusion
  1.6 0.0 copy-done
  1.6 0.5 fusion.gate_ref
  2.1 113.9 %shard_map.64 = bf16[2,384,768]{2,1,0:T(8,128)(2,1)S(1)} custom-call(s32[2,1]{1,0:T(2,128)S(1)} %copy.7.offset_ref, bf16[2,384,768]{2,1,0:T(8,128)(2,1)} %bitcast.6, bf16[2,384,768]{2,1,0:T(8,128)(2,1)} %bitcast.7, bf16[2,384,768]{2,1,0:T(8,128)(2,1)} %bitcast.8, f32[2,768]{1,0:T(2,128)S(1)} %fusion.gate_ref), custom_call_target="tpu_custom_call" | custom-call | flops 10871635968 | bytes 4718592 | tf_op jit(solution)/shard_map/pallas_call | solution.py:367
  116.0 1.0 copy.9
  (1 shorter events, 0.0 us)
Async XLA Ops:
  0.0 1.6 %copy-start = (f32[256,768]{1,0:T(8,128)S(1)}, f32[256,768]{1,0:T(8,128)}, u32[]{:S(2)}) copy-start(f32[256,768]{1,0:T(8,128)} %param.11) | copy-start | bytes 2359300

commit v4 on v3

--- a/solution.py
+++ b/solution.py
@@ -16,6 +16,7 @@
 TILE = TILE_T * TILE_H * TILE_W
 SCALE2 = math.log2(math.e) / math.sqrt(HD)
 BIG = 1e30
+AHEAD = 4
 MESH = pl.DeviceIdType.MESH
 OWN, VISIT = 0, 1
 LON, QUERY, UP, DOWN, UP2, DOWN2, BACK_LSE, BACK = range(8)
@@ -210,7 +211,8 @@
     def _():
         lax.fori_loop(0, heads, send_queries, 0)
 
-    send_first(1)
+    for h in range(1, min(AHEAD, heads)):
+        send_first(h)
     cap_copy.wait()
     forward(0)
 
@@ -277,9 +279,9 @@
     first_lane = lax.broadcasted_iota(jnp.int32, (TILE, HD), 1) == 0
 
     def step(h, carry):
-        @pl.when(h + 2 < heads)
-        def _():
-            send_first(h + 2)
+        @pl.when(h + AHEAD < heads)
+        def _():
+            send_first(h + AHEAD)
 
         query_copy(h).wait_recv()
 

time: 117 us -> 125 us (1.068)
  the two profiles are of different devices: /device:TPU:9 before, /device:TPU:1 now
where the time goes in v4:
time: 125 us
  Pallas kernels  122 us (98%)
  local copies, waits for them, and re-layouts  1.77 us (1%)
    pallas_call x1, Pallas kernels, local_loop_of_four(): pl.pallas_call(functools.partial(attention_kernel, times, heads), out_sha...  122 us

profile of v4, /device:TPU:1, one launch (start us, length us, event | category | flops | bytes accessed | tf_op | source)
XLA Modules:
  0.0 124.7 jit_solution(5281602624865390028)
XLA Ops:
  0.0 0.0 copy-start
  0.0 0.7 convert_element_type.3
  0.7 0.7 copy.7.offset_ref
  1.5 0.1 multiply_cosine_fusion
  1.6 0.0 copy-done
  1.6 0.5 fusion.gate_ref
  2.1 121.6 %shard_map.64 = bf16[2,384,768]{2,1,0:T(8,128)(2,1)S(1)} custom-call(s32[2,1]{1,0:T(2,128)S(1)} %copy.7.offset_ref, bf16[2,384,768]{2,1,0:T(8,128)(2,1)} %bitcast.6, bf16[2,384,768]{2,1,0:T(8,128)(2,1)} %bitcast.7, bf16[2,384,768]{2,1,0:T(8,128)(2,1)} %bitcast.8, f32[2,768]{1,0:T(2,128)S(1)} %fusion.gate_ref), custom_call_target="tpu_custom_call" | custom-call | flops 10871635968 | bytes 4718592 | tf_op jit(solution)/shard_map/pallas_call | solution.py:369
  123.7 1.0 copy.9
  (1 shorter events, 0.0 us)
Async XLA Ops:
  0.0 1.6 %copy-start = (f32[256,768]{1,0:T(8,128)S(1)}, f32[256,768]{1,0:T(8,128)}, u32[]{:S(2)}) copy-start(f32[256,768]{1,0:T(8,128)} %param.11) | copy-start | bytes 2359300

commit v5 on v3

--- a/solution.py
+++ b/solution.py
@@ -167,10 +167,6 @@
 
     inner = (me == 1) | (me == 2)
 
-    def send_queries(h, carry):
-        query_copy(h).start()
-        return carry
-
     def wait_queries(h, carry):
         loads(h, (2,))[0].wait()
         return carry
@@ -184,6 +180,10 @@
         def _():
             query_copy(h).start()
 
+        @pl.when(inner & (h + 2 < heads))
+        def _():
+            query_copy(h + 2).start()
+
         @pl.when(has_after)
         def _():
             up_copy(h, 0).start()
@@ -204,32 +204,37 @@
             down_copy(h, 1).start()
 
     lax.fori_loop(0, heads, wait_queries, 0)
-    send_first(0)
 
     @pl.when(inner)
     def _():
-        lax.fori_loop(0, heads, send_queries, 0)
-
-    send_first(1)
+        query_copy(0).start()
+        query_copy(1).start()
+
+    send_first(0)
     cap_copy.wait()
     forward(0)
+    send_first(1)
 
     before_cap = jnp.where(has_before, BIG, -BIG)
     after_cap = jnp.where(has_after, BIG, -BIG)
-    ones = jnp.ones((TILE, HD), jnp.bfloat16)
+    ones = jnp.ones((6 * TILE, HD), jnp.bfloat16)
     wins = [(c, w) for c in range(2) for w in range(3)]
+
+    def window(h, kind, t):
+        return jnp.concatenate([kv[h, c, kind, t + w] for c, w in wins], axis=0)
 
     def score(h, whose, t, slot):
         scaled = queries[h, whose, t].astype(jnp.float32) * SCALE2
         high = scaled.astype(jnp.bfloat16)
         low = (scaled - high.astype(jnp.float32)).astype(jnp.bfloat16)
         query = jnp.concatenate([high, low], axis=1)
-        for i, (c, w) in enumerate(wins):
-            keys = kv[h, c, 0, t + w]
-            keys = jnp.concatenate([keys, keys], axis=1)
-            scores[slot, :, i * TILE : (i + 1) * TILE] = lax.dot_general(
-                query, keys, (((1,), (1,)), ((), ())), preferred_element_type=jnp.float32
-            )
+        keys = window(h, 0, t)
+        scores[slot] = lax.dot_general(
+            query,
+            jnp.concatenate([keys, keys], axis=1),
+            (((1,), (1,)), ((), ())),
+            preferred_element_type=jnp.float32,
+        )
 
     def attend(h, whose, t, slot):
         cap_ref = cap_visit if whose == VISIT else cap_own
@@ -246,14 +251,17 @@
             ]
             tops.append(jnp.minimum(functools.reduce(jnp.maximum, part), limit))
         top = jnp.max(functools.reduce(jnp.maximum, tops), axis=1, keepdims=True)
-        total = None
-        for i, (c, w) in enumerate(wins):
+        weights = []
+        for i in range(len(wins)):
             base = jnp.maximum(top, -caps[i])
             base = jnp.concatenate([base] * (TILE // HD), axis=1)
-            weights = jnp.exp2(scores[slot, :, i * TILE : (i + 1) * TILE] - base).astype(jnp.bfloat16)
-            values = jnp.concatenate([kv[h, c, 1, t + w], ones], axis=1)
-            part = jnp.dot(weights, values, preferred_element_type=jnp.float32)
-            total = part if total is None else total + part
+            raised = jnp.exp2(scores[slot, :, i * TILE : (i + 1) * TILE] - base)
+            weights.append(raised.astype(jnp.bfloat16))
+        total = jnp.dot(
+            jnp.concatenate(weights, axis=1),
+            jnp.concatenate([window(h, 1, t), ones], axis=1),
+            preferred_element_type=jnp.float32,
+        )
         sums = total[:, HD:]
         return total[:, :HD] / sums, top + jnp.log2(sums)
 
@@ -277,10 +285,6 @@
     first_lane = lax.broadcasted_iota(jnp.int32, (TILE, HD), 1) == 0
 
     def step(h, carry):
-        @pl.when(h + 2 < heads)
-        def _():
-            send_first(h + 2)
-
         query_copy(h).wait_recv()
 
         @pl.when(has_before)
@@ -309,6 +313,10 @@
         @pl.when(h + 1 < heads)
         def _():
             forward(h + 1)
+
+        @pl.when(h + 2 < heads)
+        def _():
+            send_first(h + 2)
 
         score(h, OWN, 1, 1)
         for t in range(times):

time: 117 us -> 117 us (level)
  no operation moved by 1% of the time
where the time goes in v5:
time: 117 us
  Pallas kernels  114 us (97%)
  local copies, waits for them, and re-layouts  1.77 us (2%)
    pallas_call x1, Pallas kernels, local_loop_of_four(): pl.pallas_call(functools.partial(attention_kernel, times, heads), out_sha...  114 us

profile of v5, /device:TPU:9, one launch (start us, length us, event | category | flops | bytes accessed | tf_op | source)
XLA Modules:
  0.0 116.8 jit_solution(14023428174022023994)
XLA Ops:
  0.0 0.0 copy-start
  0.0 0.7 convert_element_type.3
  0.7 0.7 copy.7.offset_ref
  1.5 0.1 multiply_cosine_fusion
  1.6 0.0 copy-done
  1.6 0.5 fusion.gate_ref
  2.1 113.7 %shard_map.64 = bf16[2,384,768]{2,1,0:T(8,128)(2,1)S(1)} custom-call(s32[2,1]{1,0:T(2,128)S(1)} %copy.7.offset_ref, bf16[2,384,768]{2,1,0:T(8,128)(2,1)} %bitcast.6, bf16[2,384,768]{2,1,0:T(8,128)(2,1)} %bitcast.7, bf16[2,384,768]{2,1,0:T(8,128)(2,1)} %bitcast.8, f32[2,768]{1,0:T(2,128)S(1)} %fusion.gate_ref), custom_call_target="tpu_custom_call" | custom-call | flops 10871635968 | bytes 4718592 | tf_op jit(solution)/shard_map/pallas_call | solution.py:375
  115.8 1.0 copy.9
  (1 shorter events, 0.0 us)
Async XLA Ops:
  0.0 1.6 %copy-start = (f32[256,768]{1,0:T(8,128)S(1)}, f32[256,768]{1,0:T(8,128)}, u32[]{:S(2)}) copy-start(f32[256,768]{1,0:T(8,128)} %param.11) | copy-start | bytes 2359300

commit v6 on v5

--- a/solution.py
+++ b/solution.py
@@ -18,7 +18,7 @@
 BIG = 1e30
 MESH = pl.DeviceIdType.MESH
 OWN, VISIT = 0, 1
-LON, QUERY, UP, DOWN, UP2, DOWN2, BACK_LSE, BACK = range(8)
+LON, UP, DOWN, UP2, DOWN2, QUERY, BACK_LSE, BACK = 0, 1, 2, 3, 4, 5, 7, 9
 
 
 def attention_kernel(
@@ -51,7 +51,10 @@
 ):
     me = lax.axis_index("lon")
     partner = me + 1 - 2 * (me % 2)
-    across = 3 - me
+    inner = (me == 1) | (me == 2)
+    guest = 1 - inner.astype(jnp.int32)
+    hub = jnp.where(me < 2, 2, 1)
+    hub_partner = jnp.where(me < 2, 3, 0)
     place = lax.axis_index("tm")
     last = lax.axis_size("tm") - 1
     has_before, has_after = place > 0, place < last
@@ -87,7 +90,10 @@
         return remote(LON, h, kv.at[h, 0, :, inner], kv.at[h, 1, :, inner], {"lon": partner})
 
     def query_copy(h):
-        return remote(QUERY, h, queries.at[h, OWN], queries.at[h, VISIT], {"lon": across})
+        return remote(QUERY + guest, h, queries.at[h, OWN], queries.at[h, VISIT + guest], {"lon": hub})
+
+    def query_arrival(h, v):
+        return remote(QUERY + v, h, queries.at[h, OWN], queries.at[h, VISIT + v], {"lon": hub})
 
     def up_copy(h, c):
         return remote((UP, UP2)[c], h, kv.at[h, c, :, times], kv.at[h, c, :, 0], {"tm": place + 1})
@@ -95,23 +101,37 @@
     def down_copy(h, c):
         return remote((DOWN, DOWN2)[c], h, kv.at[h, c, :, 1], kv.at[h, c, :, end], {"tm": place - 1})
 
-    def back_copy(h, t):
-        return remote(BACK + t, h, o_send.at[h, t], o_back.at[h, t], {"lon": across})
-
-    def back_lse_copy(h):
-        return remote(BACK_LSE, h, lse_send.at[h], lse_back.at[h], {"lon": across})
+    def visitor(v):
+        return {"lon": (hub, hub_partner)[v]}
+
+    def back_copy(h, t, v):
+        return remote(BACK + times * v + t, h, o_send.at[h, v, t], o_back.at[h, t], visitor(v))
+
+    def back_lse_copy(h, v):
+        return remote(BACK_LSE + v, h, lse_send.at[h, v], lse_back.at[h], visitor(v))
+
+    def back_arrivals(h):
+        own_hub = {"lon": hub}
+        return [
+            remote(BACK_LSE + guest, h, lse_send.at[h, 0], lse_back.at[h], own_hub),
+            *[
+                remote(BACK + times * guest + t, h, o_send.at[h, 0, t], o_back.at[h, t], own_hub)
+                for t in range(times)
+            ],
+        ]
 
     def out_copy(h):
         return pltpu.make_async_copy(staged.at[h], out_ref.at[:, :, lanes_of(h)], out_sem.at[h])
 
-    cap_copy = pltpu.make_async_remote_copy(
-        src_ref=cap_send,
-        dst_ref=cap_visit,
-        send_sem=cap_sem.at[0],
-        recv_sem=cap_sem.at[1],
-        device_id={"lon": across},
-        device_id_type=MESH,
-    )
+    def cap_copy(v):
+        return pltpu.make_async_remote_copy(
+            src_ref=cap_send,
+            dst_ref=cap_visit.at[v],
+            send_sem=cap_sem.at[0, v],
+            recv_sem=cap_sem.at[1, v],
+            device_id={"lon": hub},
+            device_id_type=MESH,
+        )
 
     def load_all(h, carry):
         for copy in loads(h):
@@ -121,8 +141,12 @@
     lax.fori_loop(0, heads, load_all, 0)
 
     barrier = pltpu.get_barrier_semaphore()
-    for neighbour in (partner, across):
+    for neighbour in (partner, hub):
         pl.semaphore_signal(barrier, inc=1, device_id={"lon": neighbour}, device_id_type=MESH)
+
+    @pl.when(inner)
+    def _():
+        pl.semaphore_signal(barrier, inc=1, device_id={"lon": hub_partner}, device_id_type=MESH)
 
     @pl.when(has_before)
     def _():
@@ -134,7 +158,6 @@
 
     cap_own[...] = jnp.full_like(cap_own, BIG)
     cap_send[...] = jnp.full_like(cap_send, BIG)
-    across_partner = across + 1 - 2 * (across % 2)
     for t in range(times):
         shift = offset_ref[t, 0]
 
@@ -142,8 +165,8 @@
             return jnp.where(lax.rem(column - me - shift + 8, 4) == 2, -BIG, BIG)
 
         cap_own[2 * t + 1 : 2 * t + 2] = jnp.full((1, HD), cap(partner), jnp.float32)
-        cap_send[2 * t : 2 * t + 1] = jnp.full((1, HD), cap(across), jnp.float32)
-        cap_send[2 * t + 1 : 2 * t + 2] = jnp.full((1, HD), cap(across_partner), jnp.float32)
+        cap_send[2 * t : 2 * t + 1] = jnp.full((1, HD), cap(hub), jnp.float32)
+        cap_send[2 * t + 1 : 2 * t + 2] = jnp.full((1, HD), cap(hub_partner), jnp.float32)
 
     def blank(slot):
         def step(h, carry):
@@ -162,10 +185,9 @@
     def _():
         blank(end)
 
-    pl.semaphore_wait(barrier, 2 + has_before.astype(jnp.int32) + has_after.astype(jnp.int32))
-    cap_copy.start()
-
-    inner = (me == 1) | (me == 2)
+    neighbours = 2 + inner.astype(jnp.int32) + has_before.astype(jnp.int32) + has_after.astype(jnp.int32)
+    pl.semaphore_wait(barrier, neighbours)
+    cap_copy(guest).start()
 
     def wait_queries(h, carry):
         loads(h, (2,))[0].wait()
@@ -180,9 +202,9 @@
         def _():
             query_copy(h).start()
 
-        @pl.when(inner & (h + 2 < heads))
-        def _():
-            query_copy(h + 2).start()
+        @pl.when(inner & (h + 3 < heads))
+        def _():
+            query_copy(h + 3).start()
 
         @pl.when(has_after)
         def _():
@@ -209,9 +231,16 @@
     def _():
         query_copy(0).start()
         query_copy(1).start()
+        query_copy(2).start()
 
     send_first(0)
-    cap_copy.wait()
+    cap_copy(guest).wait_send()
+
+    @pl.when(inner)
+    def _():
+        for v in range(2):
+            cap_copy(v).wait_recv()
+
     forward(0)
     send_first(1)
 
@@ -237,7 +266,7 @@
         )
 
     def attend(h, whose, t, slot):
-        cap_ref = cap_visit if whose == VISIT else cap_own
+        cap_ref = cap_own if whose == OWN else cap_visit.at[whose - VISIT]
         caps, tops = [], []
         for i, (c, w) in enumerate(wins):
             limit = cap_ref[2 * t + c : 2 * t + c + 1]
@@ -266,9 +295,8 @@
         return total[:, :HD] / sums, top + jnp.log2(sums)
 
     def combine(h):
-        for t in range(times):
-            back_copy(h, t).wait_recv()
-        back_lse_copy(h).wait_recv()
+        for copy in back_arrivals(h):
+            copy.wait_recv()
         pad = jnp.zeros((HD - times, TILE), jnp.float32)
         returned = jnp.transpose(jnp.concatenate([lse_back[h], pad], axis=0))
         slot = h % 2
@@ -285,8 +313,6 @@
     first_lane = lax.broadcasted_iota(jnp.int32, (TILE, HD), 1) == 0
 
     def step(h, carry):
-        query_copy(h).wait_recv()
-
         @pl.when(has_before)
         def _():
             up_copy(h, 0).wait_recv()
@@ -298,26 +324,35 @@
             down_copy(h, 1).wait_recv()
 
         slot = h % 2
-        score(h, VISIT, 0, 0)
-        score(h, VISIT, 1, 1)
-        o0, lse0 = attend(h, VISIT, 0, 0)
-        o_send[h, 0] = o0.astype(jnp.bfloat16)
-        back_copy(h, 0).start()
+
+        @pl.when(inner)
+        def _():
+            for v in range(2):
+                query_arrival(h, v).wait_recv()
+            units = [(v, t) for v in range(2) for t in range(times)]
+            score(h, VISIT, 0, 0)
+            lses = []
+            for i, (v, t) in enumerate(units):
+                if i + 1 < len(units):
+                    score(h, VISIT + units[i + 1][0], units[i + 1][1], (i + 1) % 2)
+                o, lse = attend(h, VISIT + v, t, i % 2)
+                o_send[h, v, t] = o.astype(jnp.bfloat16)
+                back_copy(h, t, v).start()
+                lses.append(lse)
+                if t == times - 1:
+                    pair = jnp.where(first_lane, lses[-2], lses[-1])
+                    lse_send[h, v] = jnp.transpose(pair)[:times]
+                    back_lse_copy(h, v).start()
+
+        @pl.when(h + 1 < heads)
+        def _():
+            forward(h + 1)
+
+        @pl.when(h + 2 < heads)
+        def _():
+            send_first(h + 2)
+
         score(h, OWN, 0, 0)
-        o1, lse1 = attend(h, VISIT, 1, 1)
-        o_send[h, 1] = o1.astype(jnp.bfloat16)
-        lse_send[h] = jnp.transpose(jnp.where(first_lane, lse0, lse1))[:times]
-        back_copy(h, 1).start()
-        back_lse_copy(h).start()
-
-        @pl.when(h + 1 < heads)
-        def _():
-            forward(h + 1)
-
-        @pl.when(h + 2 < heads)
-        def _():
-            send_first(h + 2)
-
         score(h, OWN, 1, 1)
         for t in range(times):
             o, lse = attend(h, OWN, t, t)
@@ -335,9 +370,15 @@
 
     def finish(h, carry):
         out_copy(h).wait()
-        backs = [back_copy(h, t) for t in range(times)]
-        for copy in (lon_copy(h), query_copy(h), back_lse_copy(h), *backs):
+        for copy in (lon_copy(h), query_copy(h)):
             copy.wait_send()
+
+        @pl.when(inner)
+        def _():
+            for v in range(2):
+                back_lse_copy(h, v).wait_send()
+                for t in range(times):
+                    back_copy(h, t, v).wait_send()
 
         @pl.when(has_after)
         def _():
@@ -385,22 +426,22 @@
         out_specs=pl.BlockSpec(memory_space=pl.ANY),
         scratch_shapes=[
             pltpu.VMEM((heads, 2, 2, times + 2, TILE, HD), jnp.bfloat16),
+            pltpu.VMEM((heads, 3, times, TILE, HD), jnp.bfloat16),
+            pltpu.VMEM((2, TILE, 6 * TILE), jnp.float32),
             pltpu.VMEM((heads, 2, times, TILE, HD), jnp.bfloat16),
-            pltpu.VMEM((2, TILE, 6 * TILE), jnp.float32),
             pltpu.VMEM(per_head, jnp.bfloat16),
-            pltpu.VMEM(per_head, jnp.bfloat16),
-            pltpu.VMEM((heads, times, TILE), jnp.float32),
+            pltpu.VMEM((heads, 2, times, TILE), jnp.float32),
             pltpu.VMEM((heads, times, TILE), jnp.float32),
             pltpu.VMEM((2, times, TILE, HD), jnp.float32),
             pltpu.VMEM((2, times, TILE, HD), jnp.float32),
             pltpu.VMEM(per_head, jnp.bfloat16),
             pltpu.VMEM((8, HD), jnp.float32),
             pltpu.VMEM((8, HD), jnp.float32),
-            pltpu.VMEM((8, HD), jnp.float32),
+            pltpu.VMEM((2, 8, HD), jnp.float32),
             pltpu.SemaphoreType.DMA((3, heads)),
-            pltpu.SemaphoreType.DMA((7 + times, heads)),
-            pltpu.SemaphoreType.DMA((7 + times, heads)),
-            pltpu.SemaphoreType.DMA((2,)),
+            pltpu.SemaphoreType.DMA((9 + 2 * times, heads)),
+            pltpu.SemaphoreType.DMA((9 + 2 * times, heads)),
+            pltpu.SemaphoreType.DMA((2, 2)),
             pltpu.SemaphoreType.DMA((heads,)),
         ],
         compiler_params=pltpu.CompilerParams(

time: 117 us -> 115 us (0.983)
  the two profiles are of different devices: /device:TPU:9 before, /device:TPU:0 now
where the time goes in v6:
time: 115 us
  Pallas kernels  112 us (97%)
  local copies, waits for them, and re-layouts  1.77 us (2%)
    pallas_call x1, Pallas kernels, local_loop_of_four(): pl.pallas_call(functools.partial(attention_kernel, times, heads), out_sha...  112 us

profile of v6, /device:TPU:0, one launch (start us, length us, event | category | flops | bytes accessed | tf_op | source)
XLA Modules:
  0.0 114.9 jit_solution(17356433771822164443)
XLA Ops:
  0.0 0.0 copy-start
  0.0 0.7 convert_element_type.3
  0.7 0.7 copy.7.offset_ref
  1.5 0.1 multiply_cosine_fusion
  1.6 0.0 copy-done
  1.6 0.5 fusion.gate_ref
  2.1 111.8 %shard_map.64 = bf16[2,384,768]{2,1,0:T(8,128)(2,1)S(1)} custom-call(s32[2,1]{1,0:T(2,128)S(1)} %copy.7.offset_ref, bf16[2,384,768]{2,1,0:T(8,128)(2,1)} %bitcast.6, bf16[2,384,768]{2,1,0:T(8,128)(2,1)} %bitcast.7, bf16[2,384,768]{2,1,0:T(8,128)(2,1)} %bitcast.8, f32[2,768]{1,0:T(2,128)S(1)} %fusion.gate_ref), custom_call_target="tpu_custom_call" | custom-call | flops 10871635968 | bytes 4718592 | tf_op jit(solution)/shard_map/pallas_call | solution.py:416
  113.9 1.0 copy.9
  (1 shorter events, 0.0 us)
Async XLA Ops:
  0.0 1.6 %copy-start = (f32[256,768]{1,0:T(8,128)S(1)}, f32[256,768]{1,0:T(8,128)}, u32[]{:S(2)}) copy-start(f32[256,768]{1,0:T(8,128)} %param.11) | copy-start | bytes 2359300

commit v7 on v6

--- a/solution.py
+++ b/solution.py
@@ -329,8 +329,8 @@
         def _():
             for v in range(2):
                 query_arrival(h, v).wait_recv()
-            units = [(v, t) for v in range(2) for t in range(times)]
-            score(h, VISIT, 0, 0)
+            units = [(v, t) for v in (1, 0) for t in range(times)]
+            score(h, VISIT + units[0][0], units[0][1], 0)
             lses = []
             for i, (v, t) in enumerate(units):
                 if i + 1 < len(units):

time: 115 us -> 113 us (0.983)
  the two profiles are of different devices: /device:TPU:0 before, /device:TPU:9 now
where the time goes in v7:
time: 113 us; the launch traced here: 112 us
  Pallas kernels  109 us (96%)
  local copies, waits for them, and re-layouts  1.77 us (2%)
    pallas_call x1, Pallas kernels, local_loop_of_four(): pl.pallas_call(functools.partial(attention_kernel, times, heads), out_sha...  109 us

profile of v7, /device:TPU:9, one launch (start us, length us, event | category | flops | bytes accessed | tf_op | source)
XLA Modules:
  0.0 112.0 jit_solution(16443490364976735481)
XLA Ops:
  0.0 0.0 copy-start
  0.0 0.7 convert_element_type.3
  0.7 0.7 copy.7.offset_ref
  1.5 0.1 multiply_cosine_fusion
  1.6 0.0 copy-done
  1.6 0.5 fusion.gate_ref
  2.1 108.9 %shard_map.64 = bf16[2,384,768]{2,1,0:T(8,128)(2,1)S(1)} custom-call(s32[2,1]{1,0:T(2,128)S(1)} %copy.7.offset_ref, bf16[2,384,768]{2,1,0:T(8,128)(2,1)} %bitcast.6, bf16[2,384,768]{2,1,0:T(8,128)(2,1)} %bitcast.7, bf16[2,384,768]{2,1,0:T(8,128)(2,1)} %bitcast.8, f32[2,768]{1,0:T(2,128)S(1)} %fusion.gate_ref), custom_call_target="tpu_custom_call" | custom-call | flops 10871635968 | bytes 4718592 | tf_op jit(solution)/shard_map/pallas_call | solution.py:416
  111.0 1.0 copy.9
  (1 shorter events, 0.0 us)
Async XLA Ops:
  0.0 1.6 %copy-start = (f32[256,768]{1,0:T(8,128)S(1)}, f32[256,768]{1,0:T(8,128)}, u32[]{:S(2)}) copy-start(f32[256,768]{1,0:T(8,128)} %param.11) | copy-start | bytes 2359300
